TPU v7x, 32 devices: a whole 2x2x4 slice. The times are simulated.
32 devices in a mesh: groups: 2 (over x), fsdp: 16 (over z, y, core).
Axes of the slice: x: 2, y: 2, z: 4, core: 2. Of those that a mesh axis runs over, the one named last changes fastest.
Arguments:
- fields: bfloat16 [512, 32, 1536], P(('groups', 'fsdp')), parts along dimension 0, may hold values from -60 to 60
- shifts: int32 [2], replicated, may hold values from 1 to 7, as said below
- in_weight: bfloat16 [1536, 2304], P('fsdp'), may hold values from -0.15625 to 0.15625
- out_weight: bfloat16 [768, 1536], P('fsdp'), may hold values from -0.21875 to 0.21875
- bias_table: float32 [12, 225], replicated, may hold values from -4 to 324
- cotangent: bfloat16 [512, 32, 1536], P(('groups', 'fsdp')), parts along dimension 0, may hold values from -18 to 18
Outputs:
- attended: bfloat16 [512, 32, 1536], P(('groups', 'fsdp')), parts along dimension 0
- fields_gradient: bfloat16 [512, 32, 1536], P(('groups', 'fsdp')), parts along dimension 0
- out_grad: float32 [1536, 1536], P(('groups', 'fsdp')), parts along dimension 0
- table_grad: float32 [24, 225], P('groups'), parts along dimension 0
There are 2 independent parts, one for each index of `groups`. A program takes and returns all parts, laid end to end along the dimension named above; an argument that names none is the same for every part. Nothing has to cross between parts.
Inputs may be any that keep to these rules, and one draw needn't show every extreme that they name: The two shifts differ, and one of them is 7.
All inputs are finite; a program needn't handle non-finite values.
Results may differ from a plain program's by a relative error of at most 0.0095.
Values may be sent and summed in bfloat16 or wider, within the bound.
A program may use at most 128 MiB of HBM per device.

v0:
```python
import jax
import jax.numpy as jnp
from jax import lax
from jax.sharding import PartitionSpec as P

HEADS = 12
HD = 64
WIN = 8


def swapped(block, axis, stride):
    count = lax.axis_size(axis)
    route = []
    for low in range(count):
        high = low | 1 << stride
        if high != low and high < count:
            route += [(low, high), (high, low)]
    return lax.ppermute(block, axis, route)


def layer_norm_statistics(fields):
    values = fields.astype(jnp.float32)
    centered = values - jnp.mean(values, axis=-1, keepdims=True)
    inverse_scale = lax.rsqrt(jnp.mean(centered * centered, axis=-1, keepdims=True) + 1e-05)
    return (centered * inverse_scale, inverse_scale)


def region_labels(index, total, window, offset):
    return (index >= total - window).astype(jnp.int32) + (index >= total - offset).astype(jnp.int32)


def window_split(tensor, window):
    row_count = tensor.shape[0]
    col_count = tensor.shape[1]
    channels = tensor.shape[2]
    row_blocks = row_count // window
    col_blocks = col_count // window
    moved = tensor.reshape(row_blocks, window, col_blocks, window, channels).transpose(
        0, 2, 1, 3, 4
    )
    return moved.reshape(row_blocks * col_blocks, window * window, channels)


def window_join(tensor, window, row_count, col_count):
    channels = tensor.shape[2]
    row_blocks = row_count // window
    col_blocks = col_count // window
    moved = tensor.reshape(row_blocks, col_blocks, window, window, channels).transpose(
        0, 2, 1, 3, 4
    )
    return moved.reshape(row_count, col_count, channels)


def partner_first(tensor):
    return swapped(tensor, "fsdp", 0)


def partner_last(tensor):
    return swapped(tensor, "fsdp", 0)


def roll_forward(tensor, shift_h, shift_w):
    row_count = tensor.shape[0]
    col_count = tensor.shape[1]
    joined = jnp.concatenate([tensor, partner_first(tensor[: WIN - 1])], axis=0)
    moved = lax.dynamic_slice_in_dim(joined, shift_h, row_count, 0)
    doubled = jnp.concatenate([moved, moved], axis=1)
    return lax.dynamic_slice_in_dim(doubled, shift_w, col_count, 1)


def roll_back(tensor, shift_h, shift_w):
    row_count = tensor.shape[0]
    col_count = tensor.shape[1]
    joined = jnp.concatenate([partner_last(tensor[row_count - (WIN - 1) :]), tensor], axis=0)
    moved = lax.dynamic_slice_in_dim(joined, WIN - 1 - shift_h, row_count, 0)
    doubled = jnp.concatenate([moved, moved], axis=1)
    return lax.dynamic_slice_in_dim(doubled, col_count - shift_w, col_count, 1)


def offset_table(window):
    span = 2 * window - 1
    position = jnp.arange(window, dtype=jnp.int32)
    offset = position[:, None] - position[None, :] + window - 1
    return (offset[:, :, None] == jnp.arange(span, dtype=jnp.int32)[None, None, :]).astype(
        jnp.float32
    )


def shards(fields, shifts, in_weight, out_weight, bias_table, cotangent):
    window = WIN
    span = 2 * window - 1
    area = window * window
    row_count = fields.shape[0]
    col_count = fields.shape[1]
    width = fields.shape[2]
    windows = row_count // window * (col_count // window)
    tok_count = row_count * col_count
    inner = HEADS * HD
    score_scale = HD ** (-0.5)
    slice_rows = 2 * row_count
    row_start = lax.axis_index("fsdp") % 2 * row_count
    shift_h = shifts[0]
    shift_w = shifts[1]
    in_full, out_full = (
        lax.all_gather(in_weight, "fsdp", axis=0, tiled=True),
        lax.all_gather(out_weight, "fsdp", axis=0, tiled=True),
    )
    standardized_input, inverse_scale = layer_norm_statistics(fields)
    normalized_input = standardized_input.astype(jnp.bfloat16)
    shifted = roll_forward(normalized_input, shift_h, shift_w)
    shifted_tok = shifted.reshape(tok_count, width)
    packed = jnp.dot(shifted_tok, in_full, preferred_element_type=jnp.float32).astype(jnp.bfloat16)
    split_win = window_split(packed.reshape(row_count, col_count, 3 * inner), window).reshape(
        windows, area, 3, HEADS, HD
    )
    queries = split_win[:, :, 0]
    keyed = split_win[:, :, 1]
    valued = split_win[:, :, 2]
    table = offset_table(window)
    bias_full = jnp.einsum(
        "huv,pqu,rsv->hprqs",
        bias_table.reshape(HEADS, span, span),
        table,
        table,
        precision=lax.Precision.HIGHEST,
    ).reshape(HEADS, area, area)
    row_label = region_labels(
        row_start + jnp.arange(row_count, dtype=jnp.int32), slice_rows, window, shift_h
    )
    col_label = region_labels(jnp.arange(col_count, dtype=jnp.int32), col_count, window, shift_w)
    region = window_split(
        (3 * row_label[:, None] + col_label[None, :])[:, :, None], window
    ).reshape(windows, area)
    allowed = region[:, :, None] == region[:, None, :]
    scores = (
        jnp.einsum("nqhd,nkhd->nhqk", queries, keyed, preferred_element_type=jnp.float32)
        * score_scale
        + bias_full[None]
    )
    scores = jnp.where(allowed[:, None], scores, -1000000000.0)
    top_score = jnp.max(scores, axis=-1, keepdims=True)
    exp_scores = jnp.exp(scores - top_score)
    probability = exp_scores / jnp.sum(exp_scores, axis=-1, keepdims=True)
    prob_low = probability.astype(jnp.bfloat16)
    context = jnp.einsum(
        "nhqk,nkhd->nqhd", prob_low, valued, preferred_element_type=jnp.float32
    ).astype(jnp.bfloat16)
    context_tok = window_join(
        context.reshape(windows, area, inner), window, row_count, col_count
    ).reshape(tok_count, inner)
    projected = jnp.dot(context_tok, out_full, preferred_element_type=jnp.float32).astype(
        jnp.bfloat16
    )
    attended = roll_back(projected.reshape(row_count, col_count, width), shift_h, shift_w)
    cot_shifted = roll_forward(cotangent, shift_h, shift_w)
    cot_tok = cot_shifted.reshape(tok_count, width)
    dcontext = lax.dot_general(
        cot_tok, out_full, (((1,), (1,)), ((), ())), preferred_element_type=jnp.float32
    ).astype(jnp.bfloat16)
    dcontext_win = window_split(dcontext.reshape(row_count, col_count, inner), window).reshape(
        windows, area, HEADS, HD
    )
    dprob = jnp.einsum("nqhd,nkhd->nhqk", dcontext_win, valued, preferred_element_type=jnp.float32)
    dvalued = jnp.einsum(
        "nhqk,nqhd->nkhd", prob_low, dcontext_win, preferred_element_type=jnp.float32
    )
    dscore = probability * (dprob - jnp.sum(probability * dprob, axis=-1, keepdims=True))
    dscore_low = dscore.astype(jnp.bfloat16)
    dquery = (
        jnp.einsum("nhqk,nkhd->nqhd", dscore_low, keyed, preferred_element_type=jnp.float32)
        * score_scale
    )
    dkeyed = (
        jnp.einsum("nhqk,nqhd->nkhd", dscore_low, queries, preferred_element_type=jnp.float32)
        * score_scale
    )
    dpacked = jnp.stack([dquery, dkeyed, dvalued], axis=2).astype(jnp.bfloat16)
    dpacked_tok = window_join(
        dpacked.reshape(windows, area, 3 * inner), window, row_count, col_count
    ).reshape(tok_count, 3 * inner)
    score_local = jnp.sum(dscore, axis=0).reshape(HEADS, window, window, window, window)
    table_local = jnp.einsum(
        "hprqs,pqu,rsv->huv", score_local, table, table, precision=lax.Precision.HIGHEST
    ).reshape(HEADS, span * span)
    table_grad = lax.psum(table_local, "fsdp")
    dshifted = lax.dot_general(
        dpacked_tok, in_full, (((1,), (1,)), ((), ())), preferred_element_type=jnp.float32
    ).astype(jnp.bfloat16)
    out_term = lax.dot_general(
        context_tok, cot_tok, (((0,), (0,)), ((), ())), preferred_element_type=jnp.float32
    )
    out_grad = lax.psum_scatter(out_term, "fsdp", scatter_dimension=0, tiled=True)
    dnormed = roll_back(dshifted.reshape(row_count, col_count, width), shift_h, shift_w)
    value_gradient_rows = dnormed.astype(jnp.float32)
    average_gradient = jnp.mean(value_gradient_rows, axis=-1, keepdims=True)
    average_cross_product = jnp.mean(
        value_gradient_rows * standardized_input, axis=-1, keepdims=True
    )
    fields_gradient = (
        inverse_scale
        * (value_gradient_rows - average_gradient - standardized_input * average_cross_product)
    ).astype(jnp.bfloat16)
    return (attended, fields_gradient, out_grad, table_grad)


def solution(mesh):
    in_specs = (
        P(("groups", "fsdp"), None, None),
        P(),
        P("fsdp", None),
        P("fsdp", None),
        P(),
        P(("groups", "fsdp"), None, None),
    )
    out_specs = (
        P(("groups", "fsdp"), None, None),
        P(("groups", "fsdp"), None, None),
        P(("groups", "fsdp"), None),
        P("groups", None),
    )
    return jax.shard_map(shards, mesh=mesh, in_specs=in_specs, out_specs=out_specs, check_vma=False)
```

profile of v0, /device:TPU:0, one launch (start us, length us, event | category | flops | bytes accessed | tf_op | source)
XLA Modules:
  0.0 268.7 jit_solution(13801884071269479718)
XLA Ops:
  7.2 0.7 all-gather.3.cloned.1.call-update
  8.0 2.0 slice.41
  9.9 0.5 collective-permute-start.2
  10.4 0.3 convert_reduce_fusion.1
  10.7 0.5 fusion.8
  11.3 0.4 fusion.4
  11.7 0.9 slice.44
  12.8 0.1 reshape.117
  12.9 0.4 convolution_bitcast_fusion.1
  13.2 3.7 %convolution_bitcast_fusion = f32[12,8,8,8,8]{0,4,2,3,1:T(8,128)} fusion(f32[8,8,12,15,1]{3,1,2,0,4:T(8,128)S(1)} %convolution_bitcast_fusion.1, s32[8,8]{1,0:T(8,128)S(1)} %subtract_add_fusion), kind=kOutput, calls=%fused_computation.45 | convolution fusion | flops 8848320 | bytes 242944 | tf_op jit(solution)/shard_map/huv,pqu,rsv->hprqs/dot_general | solution.py:120
  16.9 0.6 fusion.57
  22.8 6.4 %copy.89 = f32[12,8,8,8,8]{2,1,4,3,0:T(8,128)} copy(f32[12,8,8,8,8]{0,4,2,3,1:T(8,128)} %convolution_bitcast_fusion) | data formatting | bytes 393216 | tf_op jit(solution)/shard_map/add | solution.py:136
  29.2 2.4 reshape.123
  31.7 0.7 add_bitcast_fusion
  32.4 1.4 eq.52
  35.0 1.5 broadcast_compare_fusion
  36.5 2.4 fusion.12
  38.9 2.3 fusion.18
  41.2 1.1 fusion.16
  42.3 37.3 %all-gather.3.cloned.1.call-done = bf16[1536,2304]{1,0:T(8,128)(2,1)} async-done(((bf16[96,2304]{1,0:T(8,128)(2,1)}), bf16[1536,2304]{1,0:T(8,128)(2,1)}) %all-gather.3.cloned.1.call-update) | async-done | bytes 7077904 | tf_op jit(solution)/shard_map/all_gather | solution.py:105
  79.6 7.3 %convolution_convert_fusion = bf16[512,2304]{1,0:T(8,128)(2,1)S(1)} fusion(bf16[512,1536]{1,0:T(8,128)(2,1)} %bitcast.129, bf16[1536,2304]{1,0:T(8,128)(2,1)} %all-gather.3.cloned.1.call-done), kind=kOutput, calls=%fused_computation.5 | convolution fusion | flops 3625058304 | bytes 11010048 | tf_op jit(solution)/shard_map/dot_general | solution.py:112
  87.0 1.6 copy.115
  88.5 8.2 %reshape_reshape.23 = bf16[8,64,3,12,64]{4,3,2,1,0:T(8,128)(2,1)} reshape(bf16[2,4,8,8,2304]{4,3,2,1,0:T(8,128)(2,1)} %bitcast.117) | data formatting | bytes 4718592 | tf_op jit(solution)/shard_map/reshape;reshape | solution.py:113
  96.7 6.2 %fusion.56 = (bf16[8,64,1,12,64]{4,3,2,1,0:T(8,128)(2,1)}, bf16[8,64,1,12,64]{4,3,2,1,0:T(8,128)(2,1)}, bf16[8,64,1,12,64]{4,3,2,1,0:T(8,128)(2,1)}) fusion(bf16[8,64,3,12,64]{4,3,2,1,0:T(8,128)(2,1)} %reshape_reshape.23), kind=kLoop, calls=%fused_computation.104 | loop fusion | bytes 4718592 | tf_op jit(solution)/shard_map/slice | solution.py:117
  102.9 4.4 %copy.94 = bf16[8,64,1,12,64]{1,4,3,0,2:T(8,128)(2,1)} copy(bf16[8,64,1,12,64]{4,3,2,1,0:T(8,128)(2,1)} %get-tuple-element.10) | data formatting | bytes 1572864
  107.3 6.6 %fusion.58 = (f32[8,12,64]{2,1,0:T(8,128)}, f32[8,12,64,64]{2,3,1,0:T(8,128)}) fusion(f32[12,64,64]{1,2,0:T(8,128)S(1)} %reshape.123, pred[8,64,64]{1,2,0:T(8,128)(4,1)} %broadcast_compare_fusion, bf16[8,64,1,12,64]{4,3,2,1,0:T(8,128)(2,1)} %get-tuple-element.11, bf16[8,64,1,12,64]{4,3,2,1,0:T(8,128)(2,1)} %get-tuple-element.9), kind=kOutput, calls=%fused_computation.106 | convolution fusion | flops 52297792 | bytes 3399680 | tf_op jit(solution)/shard_map/sub | solution.py:142
  113.9 4.1 %fusion.26 = bf16[8,64,12,64]{1,3,2,0:T(8,128)(2,1)} fusion(bf16[8,64,1,12,64]{1,4,3,0,2:T(8,128)(2,1)} %copy.94, f32[8,12,64,64]{2,3,1,0:T(8,128)} %get-tuple-element.15, f32[8,12,64]{2,1,0:T(8,128)} %get-tuple-element.14), kind=kOutput, calls=%fused_computation.64 | convolution fusion | flops 51511296 | bytes 3170304 | tf_op jit(solution)/shard_map/nhqk,nkhd->nqhd/dot_general | solution.py:145
  118.0 4.3 %copy.53 = bf16[8,64,12,64]{3,2,1,0:T(8,128)(2,1)} copy(bf16[8,64,12,64]{1,3,2,0:T(8,128)(2,1)} %fusion.26) | data formatting | bytes 1572864 | tf_op jit(solution)/shard_map/convert_element_type | solution.py:147
  122.3 3.9 %reshape_reshape.24 = bf16[2,4,8,8,768]{4,3,2,1,0:T(8,128)(2,1)} reshape(bf16[8,64,12,64]{3,2,1,0:T(8,128)(2,1)} %copy.53) | data formatting | bytes 1572864 | tf_op jit(solution)/shard_map/reshape;reshape | solution.py:48
  126.2 1.2 copy.54
  127.4 1.0 copy-done.4
  128.4 3.5 %fusion.59 = f32[768,1536]{1,0:T(8,128)} fusion(bf16[512,768]{1,0:T(8,128)(2,1)S(1)} %bitcast.123, bf16[512,1536]{1,0:T(8,128)(2,1)S(1)} %bitcast.119), kind=kOutput, calls=%fused_computation.107 | convolution fusion | flops 1207959552 | bytes 7077888 | tf_op jit(solution)/shard_map/dot_general | solution.py:189
  131.9 3.1 %convolution_convert_fusion.5 = bf16[512,768]{1,0:T(8,128)(2,1)S(1)} fusion(bf16[512,1536]{1,0:T(8,128)(2,1)S(1)} %bitcast.120, bf16[768,1536]{1,0:T(8,128)(2,1)} %all-gather.5.cloned.1.call-done), kind=kOutput, calls=%fused_computation.68 | convolution fusion | flops 1208352768 | bytes 4718592 | tf_op jit(solution)/shard_map/dot_general | solution.py:157
  135.1 2.2 reshape_reshape.27
  137.3 4.3 %copy.64 = bf16[8,64,12,64]{1,3,2,0:T(8,128)(2,1)} copy(bf16[8,64,12,64]{3,2,1,0:T(8,128)(2,1)} %reshape_reshape.27) | data formatting | bytes 1572864 | tf_op jit(solution)/shard_map/reshape;reshape | solution.py:160
  141.6 3.8 %multiply_reduce_fusion = (f32[8,12,64]{2,1,0:T(8,128)S(1)}, f32[8,12,64,64]{2,3,1,0:T(8,128)S(1)}) fusion(f32[8,12,64,64]{2,3,1,0:T(8,128)} %get-tuple-element.15, f32[8,12,64]{2,1,0:T(8,128)S(1)} %copy-done.11, bf16[8,64,12,64]{1,3,2,0:T(8,128)(2,1)} %copy.64, bf16[8,64,1,12,64]{1,4,3,0,2:T(8,128)(2,1)S(1)} %copy-done.7), kind=kOutput, calls=%fused_computation.28 | convolution fusion | flops 51505152 | bytes 4767744 | tf_op jit(solution)/shard_map/nqhd,nkhd->nhqk/dot_general | solution.py:163
  145.4 1.1 fusion.32
  146.5 0.6 copy-done.2
  147.1 0.8 fusion.30
  148.0 0.9 copy-done.1
  148.8 0.6 fusion.31
  149.4 0.9 copy-done.8
  150.3 1.0 fusion.29
  151.3 1.6 pad_maximum_fusion
  152.9 6.0 %copy.67 = bf16[8,64,3,12,64]{4,3,2,1,0:T(8,128)(2,1)} copy(bf16[8,64,3,12,64]{4,1,3,0,2:T(8,128)(2,1)S(1)} %pad_maximum_fusion) | data formatting | bytes 4718592 | tf_op jit(solution)/shard_map/stack | solution.py:177
  159.0 8.4 %convert_element_type.83 = bf16[2,4,8,8,2304]{4,3,2,1,0:T(8,128)(2,1)} reshape(bf16[8,64,3,12,64]{4,3,2,1,0:T(8,128)(2,1)} %copy.67) | data formatting | bytes 4718592 | tf_op jit(solution)/shard_map/convert_element_type | solution.py:177
  167.3 1.9 copy.68
  169.2 7.0 %convolution_convert_fusion.1 = bf16[512,1536]{1,0:T(8,128)(2,1)S(1)} fusion(bf16[512,2304]{1,0:T(8,128)(2,1)S(1)} %bitcast.127, bf16[1536,2304]{1,0:T(8,128)(2,1)} %all-gather.3.cloned.1.call-done), kind=kOutput, calls=%fused_computation.31 | convolution fusion | flops 3624665088 | bytes 11010048 | tf_op jit(solution)/shard_map/dot_general | solution.py:186
  176.3 1.0 slice.49
  177.3 0.3 collective-permute-start.3
  177.6 1.4 convolution_convert_fusion.2
  179.0 0.9 slice.48
  179.9 0.2 collective-permute-start.1
  180.1 2.6 reshape.124
  182.7 5.0 %copy.84 = f32[12,8,8,8,8]{4,3,1,2,0:T(8,128)} copy(f32[12,8,8,8,8]{2,1,4,3,0:T(8,128)} %reshape.124) | data formatting | bytes 393216 | tf_op jit(solution)/shard_map/reshape | solution.py:181
  187.7 4.5 %convolution_bitcast_fusion.2 = f32[15,12,8,8]{0,3,2,1:T(8,128)S(1)} fusion(f32[12,8,8,8,8]{4,3,1,2,0:T(8,128)} %copy.84, s32[8,8]{1,0:T(8,128)S(1)} %copy-done.10), kind=kOutput, calls=%fused_computation.70 | convolution fusion | flops 8848320 | bytes 242944 | tf_op jit(solution)/shard_map/hprqs,pqu,rsv->huv/dot_general | solution.py:182
  192.2 0.5 convolution_bitcast_fusion.3
  192.7 0.1 reshape.115
  192.9 59.8 %psum.7 = f32[12,225]{1,0:T(8,128)} all-reduce(f32[12,225]{1,0:T(8,128)S(1)} %reshape.115), channel_id=1, replica_groups=mesh['groups'=2,'fsdp'=16] {'fsdp'}, use_global_device_ids=true, to_apply=%region_9.10 | all-reduce | flops 2700 | bytes 21600 | tf_op jit(solution)/shard_map/psum | solution.py:185
  252.6 1.7 fusion.11
  254.3 1.7 convert_reduce_fusion
  256.1 1.4 fusion.13
  257.5 2.3 fusion.17
  259.8 2.1 fusion.7
  (48 shorter events, 0.4 us)
Async XLA Ops:
  7.2 3.2 %copy-start = (bf16[16,32,1536]{2,1,0:T(8,128)(2,1)S(1)}, bf16[16,32,1536]{2,1,0:T(8,128)(2,1)}, u32[]{:S(2)}) copy-start(bf16[16,32,1536]{2,1,0:T(8,128)(2,1)} %param.6) | copy-start | bytes 4718596
  7.2 72.5 %all-gather.3.cloned.1.call-start = ((), (), s32[]{:S(2)}) async-start(), calls=%async_computation.1 | async-start | bytes 7520256 | tf_op jit(solution)/shard_map/all_gather | solution.py:105
  7.9 124.0 %all-gather.5.cloned.1.call-start = ((), (), s32[]{:S(2)}) async-start(), calls=%async_computation.2 | async-start | bytes 2506752 | tf_op jit(solution)/shard_map/all_gather | solution.py:106
  9.9 26.6 %collective-permute-start.2 = (bf16[7,32,1536]{2,1,0:T(8,128)(2,1)}, bf16[7,32,1536]{2,1,0:T(8,128)(2,1)}, u32[]{:S(2)}, u32[]{:S(2)}) collective-permute-start(bf16[7,32,1536]{2,1,0:T(8,128)(2,1)} %slice.41), channel_id=1, source_target_pairs={{0,1},{1,0},{2,3},{3,2},{4,5},{5,4},{6,7},{7,6},{8,9},{9,8},{10,11... | collective-permute-start | bytes 2064392 | tf_op jit(solution)/shard_map/ppermute | solution.py:18
  11.3 1.5 copy-start.13
  11.7 5.2 %copy-start.14 = (s32[2]{0:T(128)S(1)}, s32[2]{0:T(128)}, u32[]{:S(2)}) copy-start(s32[2]{0:T(128)} %param.7) | copy-start | bytes 28
  12.6 23.9 %collective-permute-start = (bf16[7,32,1536]{2,1,0:T(8,128)(2,1)}, bf16[7,32,1536]{2,1,0:T(8,128)(2,1)}, u32[]{:S(2)}, u32[]{:S(2)}) collective-permute-start(bf16[7,32,1536]{2,1,0:T(8,128)(2,1)} %slice.44), channel_id=1, source_target_pairs={{0,1},{1,0},{2,3},{3,2},{4,5},{5,4},{6,7},{7,6},{8,9},{9,8},{10,11... | collective-permute-start | bytes 2064392 | tf_op jit(solution)/shard_map/ppermute | solution.py:18
  12.7 249.2 %reduce-scatter.2.cloned.1.call-start = ((), (), s32[]{:S(2)}) async-start(), calls=%async_computation.3 | async-start | bytes 5013504 | tf_op jit(solution)/shard_map/reduce_scatter | solution.py:192
  12.8 10.0 %copy-start.9 = (s32[8,8]{1,0:T(8,128)}, s32[8,8]{1,0:T(8,128)S(1)}, u32[]{:S(2)}) copy-start(s32[8,8]{1,0:T(8,128)S(1)} %subtract_add_fusion) | copy-start | bytes 772
  127.4 1.0 copy-start.4
  137.3 4.3 %copy-start.7 = (bf16[8,64,1,12,64]{1,4,3,0,2:T(8,128)(2,1)S(1)}, bf16[8,64,1,12,64]{1,4,3,0,2:T(8,128)(2,1)}, u32[]{:S(2)}) copy-start(bf16[8,64,1,12,64]{1,4,3,0,2:T(8,128)(2,1)} %copy.94) | copy-start | bytes 2359300
  137.3 4.3 %copy-start.11 = (f32[8,12,64]{2,1,0:T(8,128)S(1)}, f32[8,12,64]{2,1,0:T(8,128)}, u32[]{:S(2)}) copy-start(f32[8,12,64]{2,1,0:T(8,128)} %get-tuple-element.14) | copy-start | bytes 73732
  141.6 3.8 %copy-start.6 = (f32[8,12,64,64]{2,3,1,0:T(8,128)S(1)}, f32[8,12,64,64]{2,3,1,0:T(8,128)}, u32[]{:S(2)}) copy-start(f32[8,12,64,64]{2,3,1,0:T(8,128)} %get-tuple-element.15) | copy-start | bytes 4718596
  141.6 3.8 %copy-start.12 = (f32[8,12,64]{2,1,0:T(8,128)S(1)}, f32[8,12,64]{2,1,0:T(8,128)}, u32[]{:S(2)}) copy-start(f32[8,12,64]{2,1,0:T(8,128)} %get-tuple-element.14) | copy-start | bytes 73732
  145.4 1.7 copy-start.2
  147.1 1.7 copy-start.1
  148.8 1.5 copy-start.8
  169.2 8.4 %copy-start.5 = (bf16[2,8,4,8,768]{4,3,2,1,0:T(8,128)(2,1)S(1)}, bf16[2,8,4,8,768]{4,3,2,1,0:T(8,128)(2,1)}, u32[]{:S(2)}) copy-start(bf16[2,8,4,8,768]{4,3,2,1,0:T(8,128)(2,1)} %copy-done.4) | copy-start | bytes 2359300
  169.2 8.4 %copy-start.15 = (bf16[768,1536]{1,0:T(8,128)(2,1)S(1)}, bf16[768,1536]{1,0:T(8,128)(2,1)}, u32[]{:S(2)}) copy-start(bf16[768,1536]{1,0:T(8,128)(2,1)} %all-gather.5.cloned.1.call-done) | copy-start | bytes 7077892
  176.3 2.7 %copy-start.3 = (bf16[512,1536]{1,0:T(8,128)(2,1)}, bf16[512,1536]{1,0:T(8,128)(2,1)S(1)}, u32[]{:S(2)}) copy-start(bf16[512,1536]{1,0:T(8,128)(2,1)S(1)} %convolution_convert_fusion.1) | copy-start | bytes 4718596
  177.3 75.4 %collective-permute-start.3 = (bf16[7,32,1536]{2,1,0:T(8,128)(2,1)}, bf16[7,32,1536]{2,1,0:T(8,128)(2,1)}, u32[]{:S(2)}, u32[]{:S(2)}) collective-permute-start(bf16[7,32,1536]{2,1,0:T(8,128)(2,1)} %bitcast.31), channel_id=1, source_target_pairs={{0,1},{1,0},{2,3},{3,2},{4,5},{5,4},{6,7},{7,6},{8,9},{9,8},{10,11... | collective-permute-start | bytes 2064392 | tf_op jit(solution)/shard_map/ppermute | solution.py:18
  179.9 76.2 %collective-permute-start.1 = (bf16[7,32,1536]{2,1,0:T(8,128)(2,1)}, bf16[7,32,1536]{2,1,0:T(8,128)(2,1)}, u32[]{:S(2)}, u32[]{:S(2)}) collective-permute-start(bf16[7,32,1536]{2,1,0:T(8,128)(2,1)} %bitcast.18), channel_id=1, source_target_pairs={{0,1},{1,0},{2,3},{3,2},{4,5},{5,4},{6,7},{7,6},{8,9},{9,8},{10,11... | collective-permute-start | bytes 2064392 | tf_op jit(solution)/shard_map/ppermute | solution.py:18
  182.7 5.0 %copy-start.10 = (s32[8,8]{1,0:T(8,128)S(1)}, s32[8,8]{1,0:T(8,128)}, u32[]{:S(2)}) copy-start(s32[8,8]{1,0:T(8,128)} %copy-done.9) | copy-start | bytes 772
Sparse Core Ops, SparseCore 0:
  10.3 69.3 all-gather.2
  81.9 40.6 all-gather.4
  132.0 74.1 reduce-scatter.1
where the time goes:
time: 273 us; the launch traced here: 269 us
  local copies, waits for them, and re-layouts  79.4 us (29%)
  blocking collectives  59.8 us (22%)
  matrix products  48.2 us (18%)
  waiting for transfers between devices  38.1 us (14%)
  other arithmetic  21.3 us (8%)
  between operations  20.8 us (8%)
    psum x1, blocking collectives, shards(): table_grad = lax.psum(table_local, 'fsdp')  59.8 us
    all_gather x1, waiting for transfers between devices, shards(): lax.all_gather(in_weight, 'fsdp', axis=0, tiled=True)  37.3 us
    add x2, local copies, waits for them, and re-layouts, shards(): jnp.einsum('nqhd,nkhd->nhqk', queries, keyed, preferred_element_type=jnp....  8.81 us
    convert_element_type x1, local copies, waits for them, and re-layouts, shards(): dpacked = jnp.stack([dquery, dkeyed, dvalued], axis=2).astype(jnp.bfloat16)  8.36 us
    another operation x1, local copies, waits for them, and re-layouts, shards(): window_split(packed.reshape(row_count, col_count, 3 * inner), window)  8.21 us
    unnamed x33, local copies, waits for them, and re-layouts  7.81 us
    reshape x2, local copies, waits for them, and re-layouts, shards(): jnp.sum(dscore, axis=0).reshape(HEADS, window, window, window, window)  7.63 us
    dot_general x1, matrix products, shards(): jnp.dot(shifted_tok, in_full, preferred_element_type=jnp.float32)  7.31 us
  transfers between devices with their start and end apart: 7, of which 1 were waited for; matrix products, arithmetic and copies ran while one was open for 54% of the time, Pallas kernels for 0%

commit v1 on v0

v1 whole, which is shorter than its diff:
```python
import functools

import jax
import jax.numpy as jnp
from jax import lax
from jax.experimental import pallas as pl
from jax.experimental.pallas import tpu as pltpu
from jax.sharding import PartitionSpec as P

HEADS = 12
HD = 64
WIN = 8
SIDE = 32
MINE = HEADS // 2
HALF = MINE * HD
BAND = WIN * SIDE
PAIR = 2 * WIN * WIN
BANDS = SIDE // WIN
VMEM_LIMIT = 60 * 1024 * 1024
F32 = jnp.float32
BF16 = jnp.bfloat16


def dot(a, b, dims=((1,), (0,))):
    return lax.dot_general(a, b, (dims, ((), ())), preferred_element_type=F32)


def partner(block):
    count = lax.axis_size("fsdp")
    return lax.ppermute(block, "fsdp", [(d, d ^ 1) for d in range(count)])


def same_core_groups():
    count = lax.axis_size("fsdp")
    return [list(range(0, count, 2)), list(range(1, count, 2))]


def band_permutation(shift_w):
    t = lax.broadcasted_iota(jnp.int32, (BAND, BAND), 0)
    s = lax.broadcasted_iota(jnp.int32, (BAND, BAND), 1)
    row = (t >> 3) & 7
    col = ((t >> 6) * WIN + (t & 7) + shift_w) & (SIDE - 1)
    return (row * SIDE + col == s).astype(F32).astype(BF16)


def pair_labels(band, pair, shift_h, shift_w, axis):
    shape = (PAIR, 1) if axis == 0 else (1, PAIR)
    t = lax.broadcasted_iota(jnp.int32, shape, axis)
    which = t >> 6
    row = band * WIN + ((t >> 3) & 7)
    col = pair * 2 * WIN + which * WIN + (t & 7)

    def label(index, shift):
        return jnp.where(index >= SIDE - WIN, 1, 0) + jnp.where(index >= SIDE - shift, 1, 0)

    return which * 16 + 3 * label(row, shift_h) + label(col, shift_w)


def read_band(ref, band, shift_h):
    rows = [ref[(band * WIN + i + shift_h) & (SIDE - 1)] for i in range(WIN)]
    return jnp.concatenate(rows, axis=0)


def write_band(ref, value, band, shift_h):
    for i in range(WIN):
        ref[(band * WIN + i + shift_h) & (SIDE - 1)] = value[i * SIDE : (i + 1) * SIDE]


def forward_kernel(
    shifts, x_ref, cot_ref, w_ref, ow_ref, bias_ref, packed_ref, prob_ref, dctx_ref, proj_ref, og_ref
):
    shift_h = shifts[0]
    shift_w = shifts[1]
    perm = band_permutation(shift_w)

    def body(band, _):
        tokens = pl.ds(pl.multiple_of(band * BAND, BAND), BAND)
        xs = dot(perm, read_band(x_ref, band, shift_h)).astype(BF16)
        packed = dot(xs, w_ref[...]).astype(BF16)
        packed_ref[tokens, :] = packed
        cot = dot(perm, read_band(cot_ref, band, shift_h)).astype(BF16)
        dctx_ref[tokens, :] = dot(cot, ow_ref[...], ((1,), (1,))).astype(BF16)
        pairs = []
        for pair in range(2):
            rows = slice(pair * PAIR, (pair + 1) * PAIR)
            allowed = pair_labels(band, pair, shift_h, shift_w, 0) == pair_labels(
                band, pair, shift_h, shift_w, 1
            )
            heads = []
            for h in range(MINE):
                q = packed[rows, h * HD : (h + 1) * HD]
                k = packed[rows, HALF + h * HD : HALF + (h + 1) * HD]
                v = packed[rows, 2 * HALF + h * HD : 2 * HALF + (h + 1) * HD]
                s = dot(q, k, ((1,), (1,))) * (HD**-0.5) + bias_ref[h]
                s = jnp.where(allowed, s, -1e9)
                e = jnp.exp(s - jnp.max(s, axis=-1, keepdims=True))
                p = e / jnp.sum(e, axis=-1, keepdims=True)
                prob_ref[(band * 2 + pair) * MINE + h] = p
                heads.append(dot(p.astype(BF16), v).astype(BF16))
            pairs.append(jnp.concatenate(heads, axis=1))
        ctx = jnp.concatenate(pairs, axis=0)
        grad = dot(ctx, cot, ((0,), (0,)))

        @pl.when(band == 0)
        def _():
            og_ref[...] = grad

        @pl.when(band > 0)
        def _():
            og_ref[...] += grad

        proj = dot(ctx, ow_ref[...]).astype(BF16)
        back = dot(perm, proj, ((0,), (0,))).astype(BF16)
        write_band(proj_ref, back, band, shift_h)
        return 0

    lax.fori_loop(0, BANDS, body, 0)


def backward_kernel(shifts, packed_ref, prob_ref, dctx_ref, w_ref, dn_ref, table_ref, dpk):
    shift_h = shifts[0]
    shift_w = shifts[1]
    perm = band_permutation(shift_w)
    scale = HD**-0.5
    table_ref[...] = jnp.zeros_like(table_ref)

    def body(band, _):
        for pair in range(2):
            rows = pl.ds(pl.multiple_of(band * BAND + pair * PAIR, PAIR), PAIR)
            packed = packed_ref[rows, :]
            dctx = dctx_ref[rows, :]
            dqs, dks, dvs = [], [], []
            for h in range(MINE):
                q = packed[:, h * HD : (h + 1) * HD]
                k = packed[:, HALF + h * HD : HALF + (h + 1) * HD]
                v = packed[:, 2 * HALF + h * HD : 2 * HALF + (h + 1) * HD]
                d = dctx[:, h * HD : (h + 1) * HD]
                p = prob_ref[(band * 2 + pair) * MINE + h]
                dp = dot(d, v, ((1,), (1,)))
                dvs.append(dot(p.astype(BF16), d, ((0,), (0,))).astype(BF16))
                ds = p * (dp - jnp.sum(p * dp, axis=-1, keepdims=True))
                table_ref[h] += ds
                low = ds.astype(BF16)
                dqs.append((dot(low, k) * scale).astype(BF16))
                dks.append((dot(low, q, ((0,), (0,))) * scale).astype(BF16))
            dpk[pair * PAIR : (pair + 1) * PAIR, :] = jnp.concatenate(dqs + dks + dvs, axis=1)
        dsh = dot(dpk[...], w_ref[...], ((1,), (1,))).astype(BF16)
        back = dot(perm, dsh, ((0,), (0,))).astype(BF16)
        write_band(dn_ref, back, band, shift_h)
        return 0

    lax.fori_loop(0, BANDS, body, 0)


def norm_kernel(x_ref, o_ref):
    values = x_ref[...].astype(F32)
    centered = values - jnp.mean(values, axis=-1, keepdims=True)
    scale = lax.rsqrt(jnp.mean(centered * centered, axis=-1, keepdims=True) + 1e-05)
    o_ref[...] = (centered * scale).astype(BF16)


def norm_back_kernel(x_ref, a_ref, b_ref, o_ref):
    values = x_ref[...].astype(F32)
    centered = values - jnp.mean(values, axis=-1, keepdims=True)
    scale = lax.rsqrt(jnp.mean(centered * centered, axis=-1, keepdims=True) + 1e-05)
    xhat = centered * scale
    grad = a_ref[...].astype(F32) + b_ref[...].astype(F32)
    grad = grad.astype(BF16).astype(F32)
    mean_grad = jnp.mean(grad, axis=-1, keepdims=True)
    mean_cross = jnp.mean(grad * xhat, axis=-1, keepdims=True)
    o_ref[...] = (scale * (grad - mean_grad - xhat * mean_cross)).astype(BF16)


def rowwise(kernel, *arrays):
    rows, cols, width = arrays[0].shape
    step = 4
    spec = pl.BlockSpec((step, cols, width), lambda i: (i, 0, 0))
    return pl.pallas_call(
        kernel,
        out_shape=jax.ShapeDtypeStruct(arrays[0].shape, BF16),
        grid=(rows // step,),
        in_specs=[spec] * len(arrays),
        out_specs=spec,
        cost_estimate=pl.CostEstimate(
            flops=20 * rows * cols * width, bytes_accessed=2 * rows * cols * width * 3, transcendentals=0
        ),
    )(*arrays)


def whole(count):
    return [pl.BlockSpec(memory_space=pltpu.VMEM)] * count


def shape(dims, kind):
    return jax.ShapeDtypeStruct(dims, kind)


def offset_table(window):
    span = 2 * window - 1
    position = jnp.arange(window, dtype=jnp.int32)
    offset = position[:, None] - position[None, :] + window - 1
    return (offset[:, :, None] == jnp.arange(span, dtype=jnp.int32)[None, None, :]).astype(F32)


def both_halves(own, other, core):
    return jnp.where(
        core == 0, jnp.concatenate([own, other], axis=0), jnp.concatenate([other, own], axis=0)
    )


def shards(fields, shifts, in_weight, out_weight, bias_table, cotangent):
    row_count, col_count, width = fields.shape
    core = lax.axis_index("fsdp") % 2
    chips = lax.axis_size("fsdp") // 2
    groups = same_core_groups()
    span = 2 * WIN - 1
    area = WIN * WIN

    split = in_weight.reshape(in_weight.shape[0], 3, 2, HALF)
    keep = lax.dynamic_index_in_dim(split, core, 2, False).reshape(-1, 3 * HALF)
    give = lax.dynamic_index_in_dim(split, 1 - core, 2, False).reshape(-1, 3 * HALF)
    w_chip = both_halves(keep, partner(give), core)
    w_full = lax.all_gather(w_chip, "fsdp", axis=0, tiled=True, axis_index_groups=groups)

    mine = lax.all_gather(out_weight, "fsdp", axis=0, tiled=False, axis_index_groups=groups)
    ow_keep = lax.dynamic_slice_in_dim(mine, core * (chips // 2), chips // 2, 0)
    ow_give = lax.dynamic_slice_in_dim(mine, (1 - core) * (chips // 2), chips // 2, 0)
    ow_got = partner(ow_give)
    ow_even = jnp.where(core == 0, ow_keep, ow_got)
    ow_odd = jnp.where(core == 0, ow_got, ow_keep)
    ow_full = jnp.stack([ow_even, ow_odd], axis=1).reshape(HALF, width)

    normed = rowwise(norm_kernel, fields)
    x_all = both_halves(normed, partner(normed), core)
    cot_all = both_halves(cotangent, partner(cotangent), core)

    table = offset_table(WIN)
    own_table = lax.dynamic_slice_in_dim(bias_table, core * MINE, MINE, 0)
    bias = jnp.einsum(
        "huv,pqu,rsv->hprqs",
        own_table.reshape(MINE, span, span),
        table,
        table,
        precision=lax.Precision.HIGHEST,
    ).reshape(MINE, area, area)
    bias = jnp.tile(bias, (1, 2, 2))

    tokens = SIDE * SIDE
    blocks = BANDS * 2 * MINE
    params = pltpu.CompilerParams(vmem_limit_bytes=VMEM_LIMIT)
    smem = pl.BlockSpec(memory_space=pltpu.SMEM)
    packed, prob, dctx, proj, og = pl.pallas_call(
        forward_kernel,
        out_shape=(
            shape((tokens, 3 * HALF), BF16),
            shape((blocks, PAIR, PAIR), F32),
            shape((tokens, HALF), BF16),
            shape((SIDE, SIDE, width), BF16),
            shape((HALF, width), F32),
        ),
        in_specs=[smem] + whole(5),
        out_specs=tuple(whole(5)),
        compiler_params=params,
        cost_estimate=pl.CostEstimate(flops=10**10, bytes_accessed=2 * 10**7, transcendentals=10**6),
    )(shifts, x_all, cot_all, w_full, ow_full, bias)

    rows = og.shape[0] // chips
    parts = og.reshape(chips // 2, 2, rows, width)
    og_keep = lax.dynamic_index_in_dim(parts, core, 1, False)
    og_got = partner(lax.dynamic_index_in_dim(parts, 1 - core, 1, False))
    og_all = both_halves(og_keep, og_got, core).reshape(chips * rows, width)
    out_grad = lax.psum_scatter(
        og_all, "fsdp", scatter_dimension=0, tiled=True, axis_index_groups=groups
    )

    dn, score = pl.pallas_call(
        backward_kernel,
        out_shape=(shape((SIDE, SIDE, width), BF16), shape((MINE, PAIR, PAIR), F32)),
        in_specs=[smem] + whole(4),
        out_specs=tuple(whole(2)),
        scratch_shapes=[pltpu.VMEM((BAND, 3 * HALF), BF16)],
        compiler_params=params,
        cost_estimate=pl.CostEstimate(flops=10**10, bytes_accessed=2 * 10**7, transcendentals=10**6),
    )(shifts, packed, prob, dctx, w_full)

    def swap_rows(full):
        own = lax.dynamic_slice_in_dim(full, core * row_count, row_count, 0)
        return own, partner(lax.dynamic_slice_in_dim(full, (1 - core) * row_count, row_count, 0))

    a_own, a_got = swap_rows(proj)
    attended = (a_own.astype(F32) + a_got.astype(F32)).astype(BF16)
    d_own, d_got = swap_rows(dn)
    fields_gradient = rowwise(norm_back_kernel, fields, d_own, d_got)

    local = (score[:, :area, :area] + score[:, area:, area:]).reshape(MINE, WIN, WIN, WIN, WIN)
    own_grad = jnp.einsum(
        "hprqs,pqu,rsv->huv", local, table, table, precision=lax.Precision.HIGHEST
    ).reshape(MINE, span * span)
    padded = lax.dynamic_update_slice_in_dim(
        jnp.zeros((HEADS, span * span), F32), own_grad, core * MINE, 0
    )
    table_grad = lax.psum(padded, "fsdp")
    return (attended, fields_gradient, out_grad, table_grad)


def solution(mesh):
    in_specs = (
        P(("groups", "fsdp"), None, None),
        P(),
        P("fsdp", None),
        P("fsdp", None),
        P(),
        P(("groups", "fsdp"), None, None),
    )
    out_specs = (
        P(("groups", "fsdp"), None, None),
        P(("groups", "fsdp"), None, None),
        P(("groups", "fsdp"), None),
        P("groups", None),
    )
    return jax.shard_map(shards, mesh=mesh, in_specs=in_specs, out_specs=out_specs, check_vma=False)
```

time: 273 us -> 272 us (level); the launches traced: 269 us -> 272 us
  Pallas kernels: 0 us -> 70.1 us
  local copies, waits for them, and re-layouts: 79.4 us -> 16.3 us
  waiting for transfers between devices: 38.1 us -> 92.4 us
  matrix products: 48.2 us -> 2.88 us
  between operations: 20.8 us -> 14 us
  other arithmetic: 21.3 us -> 14.6 us
    pallas_call x0 -> x4, Pallas kernels: none -> 70.1 us  [the longest x1 36.9 us: shards(): pl.pallas_call(forward_kernel, out_shape=(shape((tokens, 3 * HALF), BF16)...]
    all_gather x2, waiting for transfers between devices: 37.4 us -> 87.7 us  [the longest x1 56.5 us: shards(): lax.all_gather(w_chip, 'fsdp', axis=0, tiled=True, axis_index_groups=groups)]
    dot_general x14 -> x4, matrix products: 41.6 us -> 2.88 us  [the longest x2 1.74 us: shards(): jnp.einsum('hprqs,pqu,rsv->huv', local, table, table, precision=lax.Preci...]
    another operation x7 -> x3, local copies, waits for them, and re-layouts: 26.2 us -> 1.89 us  [shards(): bias = jnp.tile(bias, (1, 2, 2))]
    convert_element_type x2 -> x0, local copies, waits for them, and re-layouts: 12.6 us -> none  [the longest x1 8.36 us: shards(): dpacked = jnp.stack([dquery, dkeyed, dvalued], axis=2).astype(jnp.bfloat16)]
    slice x6 -> x0, local copies, waits for them, and re-layouts: 11.5 us -> none  [the longest x1 6.17 us: shards(): keyed = split_win[:, :, 1]]
    concatenate x6 -> x0, other arithmetic: 11.2 us -> none  [the longest x2 3.39 us: roll_forward(): doubled = jnp.concatenate([moved, moved], axis=1)]
    select_n x0 -> x4, other arithmetic: none -> 10.3 us  [both_halves(): jnp.where(core == 0, jnp.concatenate([own, other], axis=0), jnp.concatena...]
  transfers between devices with their start and end apart: 7 -> 10, of which waited for: 1 -> 4; matrix products, arithmetic and copies ran while one was open for 54% -> 11% of each run, Pallas kernels for 0% -> 12%
where the time goes in v1:
time: 272 us
  waiting for transfers between devices  92.4 us (34%)
  Pallas kernels  70.1 us (26%)
  blocking collectives  59.6 us (22%)
  local copies, waits for them, and re-layouts  16.3 us (6%)
  other arithmetic  14.6 us (5%)
  between operations  14 us (5%)
  matrix products  2.88 us (1%)
    psum x1, blocking collectives, shards(): table_grad = lax.psum(padded, 'fsdp')  59.6 us
    all_gather x1, waiting for transfers between devices, shards(): lax.all_gather(w_chip, 'fsdp', axis=0, tiled=True, axis_index_groups=groups)  56.5 us
    pallas_call x1, Pallas kernels, shards(): pl.pallas_call(forward_kernel, out_shape=(shape((tokens, 3 * HALF), BF16)...  36.9 us
    all_gather x1, waiting for transfers between devices, shards(): lax.all_gather(out_weight, 'fsdp', axis=0, tiled=False, axis_index_groups...  31.2 us
    pallas_call x1, Pallas kernels, shards(): pl.pallas_call(backward_kernel, out_shape=(shape((SIDE, SIDE, width), BF1...  23.7 us
    select_n x4, other arithmetic, both_halves(): jnp.where(core == 0, jnp.concatenate([own, other], axis=0), jnp.concatena...  10.3 us
    pallas_call x2, Pallas kernels, rowwise(): pl.pallas_call(kernel, out_shape=jax.ShapeDtypeStruct(arrays[0].shape, BF...  9.54 us
  transfers between devices with their start and end apart: 10, of which 4 were waited for; matrix products, arithmetic and copies ran while one was open for 11% of the time, Pallas kernels for 12%

profile of v1, /device:TPU:0, one launch (start us, length us, event | category | flops | bytes accessed | tf_op | source)
XLA Modules:
  0.0 271.8 jit_solution(12914612922174338516)
XLA Ops:
  7.2 0.0 copy-start
  7.2 0.0 all-gather.6.cloned.1.call-start
  7.2 0.7 all-gather.6.cloned.1.call-update
  7.9 0.0 all-gather.4.cloned.1.call-start
  8.0 1.1 reshape.56
  9.1 2.8 %dynamic-slice_reduce_fusion.1 = (bf16[96,3,384]{2,1,0:T(4,128)(2,1)S(1)}, bf16[96,3,384]{2,1,0:T(4,128)(2,1)S(1)}) fusion(bf16[96,3,2,384]{3,2,1,0:T(2,128)(2,1)S(1)} %reshape.56, s32[]{:T(128)S(6)} %select_n.84, s32[]{:T(128)S(6)} %select_n.85), kind=kLoop, calls=%fused_computation.15 | loop fusion | bytes 884744 | tf_op jit(solution)/shard_map/jit(dynamic_index_in_dim)/dynamic_slice | solution.py:220
  12.0 0.5 collective-permute-start.2
  12.5 1.1 collective-permute-done.2
  13.6 0.8 maximum_select_fusion.3
  14.5 0.0 all-gather.4.cloned.1.call-update
  14.5 0.2 reduce-scatter.2.cloned.1.call-start
  14.7 4.1 %shard_map.93 = bf16[16,32,1536]{2,1,0:T(8,128)(2,1)} custom-call(bf16[16,32,1536]{2,1,0:T(8,128)(2,1)} %x_ref.3), custom_call_target="tpu_custom_call" | custom-call | flops 15728640 | bytes 4718592 | tf_op jit(solution)/shard_map/pallas_call | solution.py:178
  18.8 0.4 collective-permute-start
  19.2 0.1 collective-permute-start.1
  19.3 0.0 copy-done
  19.3 0.1 reshape.66
  19.4 0.3 convolution_bitcast_fusion.2
  19.7 0.9 convolution_bitcast_fusion
  20.6 0.2 copy.16
  20.8 0.4 tile.10
  21.2 0.0 copy-start.1
  21.2 0.3 tile.11
  21.5 1.2 tile.12.bias_ref
  22.7 31.2 %all-gather.6.cloned.1.call-done = bf16[384,1536]{1,0:T(8,128)(2,1)} async-done(((bf16[48,1536]{1,0:T(8,128)(2,1)}), bf16[384,1536]{1,0:T(8,128)(2,1)}) %all-gather.6.cloned.1.call-update) | async-done | bytes 1179664 | tf_op jit(solution)/shard_map/all_gather | solution.py:225
  53.9 1.1 constant_dynamic-slice_fusion.4
  55.0 0.1 collective-permute-start.3
  55.1 0.0 collective-permute-done
  55.1 0.0 copy-done.1
  55.1 3.4 %maximum_select_fusion.x_ref = bf16[32,32,1536]{2,1,0:T(8,128)(2,1)} fusion(bf16[16,32,1536]{2,1,0:T(8,128)(2,1)} %collective-permute-done, bf16[16,32,1536]{2,1,0:T(8,128)(2,1)S(1)} %copy-done.1, pred[]{:T(512)S(6)} %eq.41), kind=kLoop, calls=%fused_computation | loop fusion | flops 4718592 | bytes 6291457 | tf_op jit(solution)/shard_map/jit(_where)/select_n | solution.py:206
  58.5 0.0 copy-start.5
  58.5 0.0 collective-permute-done.1
  58.5 4.4 %maximum_select_fusion.1.cot_ref = bf16[32,32,1536]{2,1,0:T(8,128)(2,1)} fusion(bf16[16,32,1536]{2,1,0:T(8,128)(2,1)} %collective-permute-done.1, bf16[16,32,1536]{2,1,0:T(8,128)(2,1)} %param.11, pred[]{:T(512)S(6)} %eq.41), kind=kLoop, calls=%fused_computation.1 | loop fusion | flops 4718592 | bytes 6291457 | tf_op jit(solution)/shard_map/jit(_where)/select_n | solution.py:206
  62.9 0.0 collective-permute-done.3
  62.9 0.0 copy-done.5
  62.9 0.1 select_bitcast_fusion.1
  63.0 1.1 pad_maximum_fusion
  64.1 56.5 %all-gather.4.cloned.1.call-done.w_ref = bf16[1536,1152]{1,0:T(8,128)(2,1)} async-done(((bf16[192,1152]{1,0:T(8,128)(2,1)}), bf16[1536,1152]{1,0:T(8,128)(2,1)}) %all-gather.4.cloned.1.call-update) | async-done | bytes 3538960 | tf_op jit(solution)/shard_map/all_gather | solution.py:223
  120.6 36.9 %shard_map.94 = (bf16[1024,1152]{1,0:T(8,128)(2,1)}, f32[48,128,128]{2,1,0:T(8,128)}, bf16[1024,384]{1,0:T(8,128)(2,1)}, bf16[32,32,1536]{2,1,0:T(8,128)(2,1)}, f32[384,1536]{1,0:T(8,128)}) custom-call(s32[2]{0:T(128)} %shifts.3, bf16[32,32,1536]{2,1,0:T(8,128)(2,1)} %maximum_select_fusion.x_ref, bf16[32,32,1536]{2,1,0:T(8,128)(2,1)} %maximum_select_fusion.1.cot_ref, ...), custom_call_target="tpu_custom_call" | custom-call | flops 10000000000 | bytes 20000000 | tf_op jit(solution)/shard_map/pallas_call | solution.py:252
  157.5 1.8 dynamic-slice_bitcast_fusion.1
  159.4 0.1 collective-permute-start.6
  159.5 2.8 %collective-permute-done.6 = f32[4,48,1536]{2,1,0:T(8,128)S(1)} collective-permute-done((f32[4,48,1536]{2,1,0:T(8,128)S(1)}, f32[4,48,1536]{2,1,0:T(8,128)S(1)}, u32[]{:S(2)}, u32[]{:S(2)}) %collective-permute-start.6) | collective-permute-done | bytes 1179680 | tf_op jit(solution)/shard_map/ppermute | solution.py:30
  162.3 1.6 maximum_select_fusion.2
  163.9 0.0 reduce-scatter.2.cloned.1.call-update
  164.0 23.7 %shard_map.95 = (bf16[32,32,1536]{2,1,0:T(8,128)(2,1)}, f32[6,128,128]{2,1,0:T(8,128)}) custom-call(s32[2]{0:T(128)} %shifts.3, bf16[1024,1152]{1,0:T(8,128)(2,1)} %get-tuple-element.12.packed_ref, f32[48,128,128]{2,1,0:T(8,128)} %get-tuple-element.13.prob_ref, bf16[1024,384]{1,0:T(8,128)(2,1)} %get-tuple-element.14.dctx_ref, ...), custom_call_target="tpu_custom_call" | custom-call | flops 10000000000 | bytes 20000000 | tf_op jit(solution)/shard_map/pallas_call | solution.py:276
  187.7 0.0 copy-start.2
  187.7 4.0 %constant_dynamic-slice_fusion = (bf16[16,32,1536]{2,1,0:T(8,128)(2,1)}, bf16[16,32,1536]{2,1,0:T(8,128)(2,1)}) fusion(bf16[32,32,1536]{2,1,0:T(8,128)(2,1)} %get-tuple-element.15, s32[]{:T(128)S(6)} %select_n.94, s32[]{:T(128)S(6)} %select_n.93), kind=kLoop, calls=%fused_computation.27 | loop fusion | bytes 6291464 | tf_op jit(solution)/shard_map/dynamic_slice | solution.py:288
  191.7 0.2 collective-permute-start.5
  191.9 0.0 copy-done.2
  191.9 1.2 constant_dynamic-slice_fusion.2
  193.1 0.3 collective-permute-start.4
  193.5 0.0 copy-done.6
  193.5 0.1 slice_add_fusion
  193.6 0.4 reshape.62
  194.1 1.4 convolution_bitcast_fusion.1
  195.5 0.3 convolution_bitcast_fusion.3
  195.8 0.1 reshape.63
  195.9 0.2 dynamic_update_slice.3
  196.1 59.6 %psum.7 = f32[12,225]{1,0:T(8,128)} all-reduce(f32[12,225]{1,0:T(8,128)S(1)} %dynamic_update_slice.3), channel_id=1, replica_groups=mesh['groups'=2,'fsdp'=16] {'fsdp'}, use_global_device_ids=true, to_apply=%region_1.2 | all-reduce | flops 2700 | bytes 21600 | tf_op jit(solution)/shard_map/psum | solution.py:302
  255.7 0.0 collective-permute-done.5.b_ref
  255.7 1.2 copy-done.4
  256.8 5.4 %shard_map.96 = bf16[16,32,1536]{2,1,0:T(8,128)(2,1)} custom-call(bf16[16,32,1536]{2,1,0:T(8,128)(2,1)} %x_ref.3, bf16[16,32,1536]{2,1,0:T(8,128)(2,1)} %get-tuple-element.21.a_ref, bf16[16,32,1536]{2,1,0:T(8,128)(2,1)} %copy-done.4), custom_call_target="tpu_custom_call" | custom-call | flops 15728640 | bytes 4718592 | tf_op jit(solution)/shard_map/pallas_call | solution.py:178
  262.3 0.0 collective-permute-done.4
  262.3 0.0 copy-done.3
  262.3 3.0 %add_convert_fusion = bf16[16,32,1536]{2,1,0:T(8,128)(2,1)} fusion(bf16[16,32,1536]{2,1,0:T(8,128)(2,1)} %collective-permute-done.4, bf16[32,32,1536]{2,1,0:T(8,128)(2,1)S(1)} %copy-done.3, s32[]{:T(128)S(6)} %select_n.93), kind=kLoop, calls=%fused_computation.2 | loop fusion | flops 3145728 | bytes 4718596 | tf_op jit(solution)/shard_map/convert_element_type | solution.py:291
  (9 shorter events, 0.1 us)
Async XLA Ops:
  7.2 12.2 %copy-start = (f32[12,225]{1,0:T(8,128)S(1)}, f32[12,225]{1,0:T(8,128)}, u32[]{:S(2)}) copy-start(f32[12,225]{1,0:T(8,128)} %param.10) | copy-start | bytes 32404
  7.2 46.7 %all-gather.6.cloned.1.call-start = ((), (), s32[]{:S(2)}) async-start(), calls=%async_computation.3 | async-start | bytes 1327104 | tf_op jit(solution)/shard_map/all_gather | solution.py:225
  7.9 112.7 %all-gather.4.cloned.1.call-start = ((), (), s32[]{:S(2)}) async-start(), calls=%async_computation.1 | async-start | bytes 3981312 | tf_op jit(solution)/shard_map/all_gather | solution.py:223
  12.0 1.6 collective-permute-start.2
  14.5 250.8 %reduce-scatter.2.cloned.1.call-start = ((), (), s32[]{:S(2)}) async-start(), calls=%async_computation.2 | async-start | bytes 2654208 | tf_op jit(solution)/shard_map/reduce_scatter | solution.py:272
  18.8 36.3 %collective-permute-start = (bf16[16,32,1536]{2,1,0:T(8,128)(2,1)}, bf16[16,32,1536]{2,1,0:T(8,128)(2,1)}, u32[]{:S(2)}, u32[]{:S(2)}) collective-permute-start(bf16[16,32,1536]{2,1,0:T(8,128)(2,1)} %shard_map.93), channel_id=1, source_target_pairs={{0,1},{1,0},{2,3},{3,2},{4,5},{5,4},{6,7},{7,6},{8,9},{9,8},{10,11... | collective-permute-start | bytes 4718600 | tf_op jit(solution)/shard_map/ppermute | solution.py:30
  19.2 39.3 %collective-permute-start.1 = (bf16[16,32,1536]{2,1,0:T(8,128)(2,1)}, bf16[16,32,1536]{2,1,0:T(8,128)(2,1)}, u32[]{:S(2)}, u32[]{:S(2)}) collective-permute-start(bf16[16,32,1536]{2,1,0:T(8,128)(2,1)} %param.11), channel_id=1, source_target_pairs={{0,1},{1,0},{2,3},{3,2},{4,5},{5,4},{6,7},{7,6},{8,9},{9,8},{10,11... | collective-permute-start | bytes 4718600 | tf_op jit(solution)/shard_map/ppermute | solution.py:30
  21.2 33.9 %copy-start.1 = (bf16[16,32,1536]{2,1,0:T(8,128)(2,1)S(1)}, bf16[16,32,1536]{2,1,0:T(8,128)(2,1)}, u32[]{:S(2)}) copy-start(bf16[16,32,1536]{2,1,0:T(8,128)(2,1)} %shard_map.93) | copy-start | bytes 4718596
  55.0 7.9 %collective-permute-start.3 = (bf16[4,48,1536]{2,1,0:T(8,128)(2,1)S(1)}, bf16[4,48,1536]{2,1,0:T(8,128)(2,1)S(1)}, u32[]{:S(2)}, u32[]{:S(2)}) collective-permute-start(bf16[4,48,1536]{2,1,0:T(8,128)(2,1)S(1)} %constant_dynamic-slice_fusion.4), channel_id=1, source_target_pairs={{0,1},{1,0},{2,3},{3,2},{4,5},{5,4},{6,7},{7,6},{8,9},{9,8},{10,11... | collective-permute-start | bytes 1769480 | tf_op jit(solution)/shard_map/ppermute | solution.py:30
  58.5 4.4 %copy-start.5 = (bf16[384,1536]{1,0:T(8,128)(2,1)S(1)}, bf16[384,1536]{1,0:T(8,128)(2,1)}, u32[]{:S(2)}) copy-start(bf16[384,1536]{1,0:T(8,128)(2,1)} %all-gather.6.cloned.1.call-done) | copy-start | bytes 3538948
  159.4 2.9 %collective-permute-start.6 = (f32[4,48,1536]{2,1,0:T(8,128)S(1)}, f32[4,48,1536]{2,1,0:T(8,128)S(1)}, u32[]{:S(2)}, u32[]{:S(2)}) collective-permute-start(f32[4,48,1536]{2,1,0:T(8,128)S(1)} %get-tuple-element.23), channel_id=1, source_target_pairs={{0,1},{1,0},{2,3},{3,2},{4,5},{5,4},{6,7},{7,6},{8,9},{9,8},{10,11... | collective-permute-start | bytes 3538952 | tf_op jit(solution)/shard_map/ppermute | solution.py:30
  187.7 4.2 %copy-start.2 = (bf16[32,32,1536]{2,1,0:T(8,128)(2,1)S(1)}, bf16[32,32,1536]{2,1,0:T(8,128)(2,1)}, u32[]{:S(2)}) copy-start(bf16[32,32,1536]{2,1,0:T(8,128)(2,1)} %get-tuple-element.11) | copy-start | bytes 9437188
  191.7 63.9 %collective-permute-start.5 = (bf16[16,32,1536]{2,1,0:T(8,128)(2,1)}, bf16[16,32,1536]{2,1,0:T(8,128)(2,1)S(1)}, u32[]{:S(2)}, u32[]{:S(2)}) collective-permute-start(bf16[16,32,1536]{2,1,0:T(8,128)(2,1)} %get-tuple-element.20), channel_id=1, source_target_pairs={{0,1},{1,0},{2,3},{3,2},{4,5},{5,4},{6,7},{7,6},{8,9},{9,8},{10,11... | collective-permute-start | bytes 4718600 | tf_op jit(solution)/shard_map/ppermute | solution.py:30
  191.9 1.6 copy-start.6
  193.1 69.1 %collective-permute-start.4 = (bf16[16,32,1536]{2,1,0:T(8,128)(2,1)}, bf16[16,32,1536]{2,1,0:T(8,128)(2,1)}, u32[]{:S(2)}, u32[]{:S(2)}) collective-permute-start(bf16[16,32,1536]{2,1,0:T(8,128)(2,1)} %constant_dynamic-slice_fusion.2), channel_id=1, source_target_pairs={{0,1},{1,0},{2,3},{3,2},{4,5},{5,4},{6,7},{7,6},{8,9},{9,8},{10,11... | collective-permute-start | bytes 4718600 | tf_op jit(solution)/shard_map/ppermute | solution.py:30
  255.7 1.2 copy-start.4
  256.8 5.4 %copy-start.3 = (bf16[32,32,1536]{2,1,0:T(8,128)(2,1)S(1)}, bf16[32,32,1536]{2,1,0:T(8,128)(2,1)}, u32[]{:S(2)}) copy-start(bf16[32,32,1536]{2,1,0:T(8,128)(2,1)} %get-tuple-element.11) | copy-start | bytes 9437188
Sparse Core Ops, SparseCore 0:
  10.2 43.6 all-gather.5
  56.7 63.9 all-gather.3
  164.1 67.6 reduce-scatter.1

commit v2 on v1

--- a/solution.py
+++ b/solution.py
@@ -61,17 +61,30 @@
     return jnp.concatenate(rows, axis=0)
 
 
-def write_band(ref, value, band, shift_h):
+def write_band(own_ref, give_ref, value, band, shift_h, core):
+    half = SIDE // 2
     for i in range(WIN):
-        ref[(band * WIN + i + shift_h) & (SIDE - 1)] = value[i * SIDE : (i + 1) * SIDE]
+        row = (band * WIN + i + shift_h) & (SIDE - 1)
+        inside = row & (half - 1)
+        mine = row // half == core
+
+        @pl.when(mine)
+        def _():
+            own_ref[inside] = value[i * SIDE : (i + 1) * SIDE]
+
+        @pl.when(jnp.logical_not(mine))
+        def _():
+            give_ref[inside] = value[i * SIDE : (i + 1) * SIDE]
 
 
 def forward_kernel(
-    shifts, x_ref, cot_ref, w_ref, ow_ref, bias_ref, packed_ref, prob_ref, dctx_ref, proj_ref, og_ref
+    shifts, x_ref, cot_ref, w_ref, ow_ref, bias_ref, packed_ref, prob_ref, dctx_ref, own_ref, give_ref, og_out, og_ref
 ):
     shift_h = shifts[0]
     shift_w = shifts[1]
+    core = shifts[2]
     perm = band_permutation(shift_w)
+    ow = ow_ref.at[pl.ds(pl.multiple_of(core * HALF, HALF), HALF), :]
 
     def body(band, _):
         tokens = pl.ds(pl.multiple_of(band * BAND, BAND), BAND)
@@ -79,7 +92,7 @@
         packed = dot(xs, w_ref[...]).astype(BF16)
         packed_ref[tokens, :] = packed
         cot = dot(perm, read_band(cot_ref, band, shift_h)).astype(BF16)
-        dctx_ref[tokens, :] = dot(cot, ow_ref[...], ((1,), (1,))).astype(BF16)
+        dctx_ref[tokens, :] = dot(cot, ow[...], ((1,), (1,))).astype(BF16)
         pairs = []
         for pair in range(2):
             rows = slice(pair * PAIR, (pair + 1) * PAIR)
@@ -103,21 +116,29 @@
 
         @pl.when(band == 0)
         def _():
-            og_ref[...] = grad
+            og_ref[...] = grad.reshape(og_ref.shape)
 
         @pl.when(band > 0)
         def _():
-            og_ref[...] += grad
-
-        proj = dot(ctx, ow_ref[...]).astype(BF16)
+            og_ref[...] += grad.reshape(og_ref.shape)
+
+        proj = dot(ctx, ow[...]).astype(BF16)
         back = dot(perm, proj, ((0,), (0,))).astype(BF16)
-        write_band(proj_ref, back, band, shift_h)
+        write_band(own_ref, give_ref, back, band, shift_h, core)
         return 0
 
     lax.fori_loop(0, BANDS, body, 0)
-
-
-def backward_kernel(shifts, packed_ref, prob_ref, dctx_ref, w_ref, dn_ref, table_ref, dpk):
+    parts, rows, _ = og_out.shape
+
+    def order(i, _):
+        owner = lax.rem(shifts[3] + i, parts)
+        og_out[i] = og_ref[owner].astype(BF16)
+        return 0
+
+    lax.fori_loop(0, parts, order, 0)
+
+
+def backward_kernel(shifts, packed_ref, prob_ref, dctx_ref, w_ref, own_ref, give_ref, table_ref, dpk):
     shift_h = shifts[0]
     shift_w = shifts[1]
     perm = band_permutation(shift_w)
@@ -146,7 +167,7 @@
             dpk[pair * PAIR : (pair + 1) * PAIR, :] = jnp.concatenate(dqs + dks + dvs, axis=1)
         dsh = dot(dpk[...], w_ref[...], ((1,), (1,))).astype(BF16)
         back = dot(perm, dsh, ((0,), (0,))).astype(BF16)
-        write_band(dn_ref, back, band, shift_h)
+        write_band(own_ref, give_ref, back, band, shift_h, shifts[2])
         return 0
 
     lax.fori_loop(0, BANDS, body, 0)
@@ -208,31 +229,219 @@
     )
 
 
-def shards(fields, shifts, in_weight, out_weight, bias_table, cotangent):
+MESH = pl.DeviceIdType.MESH
+
+
+def ring_place(chip):
+    z = chip // 2
+    return jnp.where(chip % 2 == 0, z, 7 - z)
+
+
+def ring_chip(place):
+    place = (place + 8) % 8
+    return jnp.where(place < 4, 2 * place, 2 * (7 - place) + 1)
+
+
+def gather_kernel(
+    w_ref, ow_ref, x_ref, cot_ref, w_out, ow_out, x_out, cot_out, normed,
+    tok_send, tok_recv, local, pair_send, pair_recv, ring_send, ring_recv, cross_send, cross_recv,
+):
+    me = lax.axis_index("fsdp")
+    group = lax.axis_index("groups")
+    core = me % 2
+    chip = me // 2
+    place = ring_place(chip)
+    right = ring_chip(place + 1) * 2 + core
+    left = ring_chip(place - 1) * 2 + core
+    other = chip * 2 + (1 - core)
+
+    barrier = pltpu.get_barrier_semaphore()
+    for target in ({"fsdp": other}, {"fsdp": right}, {"fsdp": left}, {"groups": 1 - group}):
+        pl.semaphore_signal(barrier, inc=1, device_id=target, device_id_type=MESH)
+    pl.semaphore_wait(barrier, 4)
+
+    def remote(src, dst, send, recv, target):
+        return pltpu.make_async_remote_copy(
+            src_ref=src, dst_ref=dst, send_sem=send, recv_sem=recv, device_id=target, device_id_type=MESH
+        )
+
+    rows = w_ref.shape[0]
+    own_rows = pl.ds(pl.multiple_of((chip * 2 + core) * rows, rows), rows)
+    pairs, locals_ = [], []
+    for kind in range(3):
+        dst = w_out.at[own_rows, pl.ds(kind * HALF, HALF)]
+
+        def columns(which):
+            return w_ref.at[:, pl.ds(pl.multiple_of(kind * 2 * HALF + which * HALF, HALF), HALF)]
+
+        pairs.append(
+            remote(columns(1 - core), dst, pair_send.at[kind], pair_recv.at[kind], {"fsdp": other})
+        )
+        locals_.append(pltpu.make_async_copy(columns(core), dst, local.at[kind]))
+    locals_.append(pltpu.make_async_copy(ow_ref, ow_out.at[chip, core], local.at[3]))
+    for copy in pairs + locals_:
+        copy.start()
+    cot_far = remote(cot_ref, cot_out.at[core], tok_send.at[0], tok_recv.at[0], {"fsdp": other})
+    cot_near = pltpu.make_async_copy(cot_ref, cot_out.at[core], local.at[4])
+    for copy in locals_:
+        copy.wait()
+    for copy in pairs:
+        copy.wait()
+
+    third = 2 * rows // 3
+    thin = ow_ref.shape[0] // 3
+
+    def piece(name, chunk):
+        part = group if name[1] == "m" else 2
+        if name[0] == "w":
+            start = pl.multiple_of(chunk * (2 * rows) + part * third, third)
+            return w_out.at[pl.ds(start, third), :]
+        return ow_out.at[chunk, core, pl.ds(pl.multiple_of(part * thin, thin), thin), :]
+
+    names = ("wm", "wc", "om", "oc")
+
+    def carried(way, step):
+        if step < 4:
+            return names
+        return ("wm", "om") if way == 0 else ("wc", "oc")
+
+    def hop(way, step, name):
+        chunk = ring_chip(place - (step - 1) if way == 0 else place + (step - 1))
+        ref = piece(name, chunk)
+        i = names.index(name)
+        return remote(
+            ref, ref, ring_send.at[way, step - 1, i], ring_recv.at[way, step - 1, i],
+            {"fsdp": right if way == 0 else left},
+        )
+
+    def arrival(way, step, name):
+        chunk = ring_chip(place - step if way == 0 else place + step)
+        ref = piece(name, chunk)
+        i = names.index(name)
+        return remote(
+            ref, ref, ring_send.at[way, step - 1, i], ring_recv.at[way, step - 1, i],
+            {"fsdp": right if way == 0 else left},
+        )
+
+    def cross(way, step, name, mine):
+        chunk = ring_chip(place - step if way == 0 else place + step)
+        part = group if mine else 1 - group
+        if name == "wm":
+            start = pl.multiple_of(chunk * (2 * rows) + part * third, third)
+            ref = w_out.at[pl.ds(start, third), :]
+        else:
+            ref = ow_out.at[chunk, core, pl.ds(pl.multiple_of(part * thin, thin), thin), :]
+        i = 0 if name == "wm" else 1
+        return remote(
+            ref, ref, cross_send.at[way, step - 1, i], cross_recv.at[way, step - 1, i],
+            {"groups": 1 - group},
+        )
+
+    for name in names:
+        for way in range(2):
+            hop(way, 1, name).start()
+    cot_far.start()
+    cot_near.start()
+
+    def norm_row(i, _):
+        values = x_ref[i].astype(F32)
+        centered = values - jnp.mean(values, axis=-1, keepdims=True)
+        scale = lax.rsqrt(jnp.mean(centered * centered, axis=-1, keepdims=True) + 1e-05)
+        normed[i] = (centered * scale).astype(BF16)
+        return 0
+
+    lax.fori_loop(0, x_ref.shape[0], norm_row, 0)
+    x_far = remote(normed, x_out.at[core], tok_send.at[1], tok_recv.at[1], {"fsdp": other})
+    x_near = pltpu.make_async_copy(normed, x_out.at[core], local.at[5])
+    x_far.start()
+    x_near.start()
+
+    crossed = []
+    for step in range(1, 5):
+        for name in names:
+            for way in range(2):
+                if name not in carried(way, step):
+                    continue
+                arrival(way, step, name).wait_recv()
+                if step < 4 and name in carried(way, step + 1):
+                    hop(way, step + 1, name).start()
+                if name[1] == "m":
+                    cross(way, step, name, True).start()
+                    crossed.append((way, step, name))
+    for way, step, name in crossed:
+        cross(way, step, name, False).wait_recv()
+    half = ow_out.shape[0] // 2
+    give = ow_out.at[pl.ds((1 - core) * half, half), core]
+    swap = remote(give, give, pair_send.at[3], pair_recv.at[3], {"fsdp": other})
+    swap.start()
+    for step in range(1, 5):
+        for way in range(2):
+            for name in carried(way, step):
+                hop(way, step, name).wait_send()
+    for way, step, name in crossed:
+        cross(way, step, name, True).wait_send()
+    cot_far.wait()
+    cot_near.wait()
+    x_far.wait()
+    x_near.wait()
+    swap.wait()
+
+
+def gathered(fields, in_weight, out_weight, cotangent):
     row_count, col_count, width = fields.shape
+    count = lax.axis_size("fsdp")
+    anywhere = pl.BlockSpec(memory_space=pl.ANY)
+    dma = pltpu.SemaphoreType.DMA
+    return pl.pallas_call(
+        gather_kernel,
+        out_shape=(
+            shape((width, 3 * HALF), BF16),
+            shape((count // 2, 2, out_weight.shape[0], width), BF16),
+            shape((2, row_count, col_count, width), BF16),
+            shape((2, row_count, col_count, width), BF16),
+        ),
+        in_specs=[anywhere, anywhere, pl.BlockSpec(memory_space=pltpu.VMEM), anywhere],
+        out_specs=(anywhere,) * 4,
+        scratch_shapes=[
+            pltpu.VMEM(fields.shape, BF16),
+            dma((2,)), dma((2,)), dma((6,)), dma((4,)), dma((4,)),
+            dma((2, 4, 4)), dma((2, 4, 4)), dma((2, 4, 2)), dma((2, 4, 2)),
+        ],
+        compiler_params=pltpu.CompilerParams(
+            collective_id=0, has_side_effects=True, vmem_limit_bytes=56 * 1024 * 1024
+        ),
+        cost_estimate=pl.CostEstimate(flops=10**8, bytes_accessed=10**8, transcendentals=0),
+    )(in_weight, out_weight, fields, cotangent)
+
+
+def gathered_plain(fields, in_weight, out_weight, cotangent):
     core = lax.axis_index("fsdp") % 2
-    chips = lax.axis_size("fsdp") // 2
     groups = same_core_groups()
-    span = 2 * WIN - 1
-    area = WIN * WIN
-
     split = in_weight.reshape(in_weight.shape[0], 3, 2, HALF)
     keep = lax.dynamic_index_in_dim(split, core, 2, False).reshape(-1, 3 * HALF)
     give = lax.dynamic_index_in_dim(split, 1 - core, 2, False).reshape(-1, 3 * HALF)
     w_chip = both_halves(keep, partner(give), core)
     w_full = lax.all_gather(w_chip, "fsdp", axis=0, tiled=True, axis_index_groups=groups)
-
-    mine = lax.all_gather(out_weight, "fsdp", axis=0, tiled=False, axis_index_groups=groups)
-    ow_keep = lax.dynamic_slice_in_dim(mine, core * (chips // 2), chips // 2, 0)
-    ow_give = lax.dynamic_slice_in_dim(mine, (1 - core) * (chips // 2), chips // 2, 0)
-    ow_got = partner(ow_give)
-    ow_even = jnp.where(core == 0, ow_keep, ow_got)
-    ow_odd = jnp.where(core == 0, ow_got, ow_keep)
-    ow_full = jnp.stack([ow_even, ow_odd], axis=1).reshape(HALF, width)
-
+    ow_all = lax.all_gather(out_weight, "fsdp", axis=0, tiled=True)
     normed = rowwise(norm_kernel, fields)
     x_all = both_halves(normed, partner(normed), core)
     cot_all = both_halves(cotangent, partner(cotangent), core)
+    return w_full, ow_all, x_all, cot_all
+
+
+def shards(fields, shifts, in_weight, out_weight, bias_table, cotangent):
+    row_count, col_count, width = fields.shape
+    core = lax.axis_index("fsdp") % 2
+    chips = lax.axis_size("fsdp") // 2
+    span = 2 * WIN - 1
+    area = WIN * WIN
+
+    gather = gathered if 2 * chips == 16 else gathered_plain
+    w_full, ow_all, x_all, cot_all = gather(fields, in_weight, out_weight, cotangent)
+    ow_full = ow_all.reshape(2 * HALF, width)
+    x_all = x_all.reshape(SIDE, col_count, width)
+    cot_all = cot_all.reshape(SIDE, col_count, width)
+    scalars = jnp.concatenate([shifts, jnp.stack([core, lax.axis_index("fsdp") // 2])]).astype(jnp.int32)
 
     table = offset_table(WIN)
     own_table = lax.dynamic_slice_in_dim(bias_table, core * MINE, MINE, 0)
@@ -249,48 +458,49 @@
     blocks = BANDS * 2 * MINE
     params = pltpu.CompilerParams(vmem_limit_bytes=VMEM_LIMIT)
     smem = pl.BlockSpec(memory_space=pltpu.SMEM)
-    packed, prob, dctx, proj, og = pl.pallas_call(
+    packed, prob, dctx, a_own, a_give, og = pl.pallas_call(
         forward_kernel,
         out_shape=(
             shape((tokens, 3 * HALF), BF16),
             shape((blocks, PAIR, PAIR), F32),
             shape((tokens, HALF), BF16),
-            shape((SIDE, SIDE, width), BF16),
-            shape((HALF, width), F32),
+            shape(fields.shape, BF16),
+            shape(fields.shape, BF16),
+            shape((chips, HALF // chips, width), BF16),
         ),
         in_specs=[smem] + whole(5),
-        out_specs=tuple(whole(5)),
+        out_specs=tuple(whole(6)),
+        scratch_shapes=[pltpu.VMEM((chips, HALF // chips, width), F32)],
         compiler_params=params,
         cost_estimate=pl.CostEstimate(flops=10**10, bytes_accessed=2 * 10**7, transcendentals=10**6),
-    )(shifts, x_all, cot_all, w_full, ow_full, bias)
-
-    rows = og.shape[0] // chips
-    parts = og.reshape(chips // 2, 2, rows, width)
-    og_keep = lax.dynamic_index_in_dim(parts, core, 1, False)
-    og_got = partner(lax.dynamic_index_in_dim(parts, 1 - core, 1, False))
-    og_all = both_halves(og_keep, og_got, core).reshape(chips * rows, width)
-    out_grad = lax.psum_scatter(
-        og_all, "fsdp", scatter_dimension=0, tiled=True, axis_index_groups=groups
-    )
-
-    dn, score = pl.pallas_call(
+    )(scalars, x_all, cot_all, w_full, ow_full, bias)
+
+    terms = []
+    for far in range(chips):
+        route = [
+            (2 * c + k, k * chips + (c + far) % chips) for c in range(chips) for k in range(2)
+        ]
+        terms.append(lax.ppermute(og[far], "fsdp", route))
+    a_got = partner(a_give)
+
+    d_own, d_give, score = pl.pallas_call(
         backward_kernel,
-        out_shape=(shape((SIDE, SIDE, width), BF16), shape((MINE, PAIR, PAIR), F32)),
+        out_shape=(
+            shape(fields.shape, BF16),
+            shape(fields.shape, BF16),
+            shape((MINE, PAIR, PAIR), F32),
+        ),
         in_specs=[smem] + whole(4),
-        out_specs=tuple(whole(2)),
+        out_specs=tuple(whole(3)),
         scratch_shapes=[pltpu.VMEM((BAND, 3 * HALF), BF16)],
         compiler_params=params,
         cost_estimate=pl.CostEstimate(flops=10**10, bytes_accessed=2 * 10**7, transcendentals=10**6),
-    )(shifts, packed, prob, dctx, w_full)
-
-    def swap_rows(full):
-        own = lax.dynamic_slice_in_dim(full, core * row_count, row_count, 0)
-        return own, partner(lax.dynamic_slice_in_dim(full, (1 - core) * row_count, row_count, 0))
-
-    a_own, a_got = swap_rows(proj)
+    )(scalars, packed, prob, dctx, w_full)
+
+    d_got = partner(d_give)
     attended = (a_own.astype(F32) + a_got.astype(F32)).astype(BF16)
-    d_own, d_got = swap_rows(dn)
     fields_gradient = rowwise(norm_back_kernel, fields, d_own, d_got)
+    out_grad = functools.reduce(jnp.add, [term.astype(F32) for term in terms])
 
     local = (score[:, :area, :area] + score[:, area:, area:]).reshape(MINE, WIN, WIN, WIN, WIN)
     own_grad = jnp.einsum(
@@ -299,7 +509,12 @@
     padded = lax.dynamic_update_slice_in_dim(
         jnp.zeros((HEADS, span * span), F32), own_grad, core * MINE, 0
     )
-    table_grad = lax.psum(padded, "fsdp")
+    table_grad = padded
+    count, stride = 2 * chips, 1
+    while stride < count:
+        route = [(d, d ^ stride) for d in range(count)]
+        table_grad = table_grad + lax.ppermute(table_grad, "fsdp", route)
+        stride *= 2
     return (attended, fields_gradient, out_grad, table_grad)
 
 

time: 272 us -> 192 us (0.71)
  waiting for transfers between devices: 92.4 us -> 15.5 us
  Pallas kernels: 70.1 us -> 135 us
  blocking collectives: 59.6 us -> 0 us
  starting transfers between devices: 1.98 us -> 28.1 us
  between operations: 14 us -> 0.93 us
  local copies, waits for them, and re-layouts: 16.3 us -> 5.09 us
  other arithmetic: 14.6 us -> 4.9 us
    all_gather x2 -> x0, waiting for transfers between devices: 87.7 us -> none  [the longest x1 56.5 us: shards(): lax.all_gather(w_chip, 'fsdp', axis=0, tiled=True, axis_index_groups=groups)]
    pallas_call x1 -> x2, Pallas kernels: 23.7 us -> 90.7 us  [the longest x1 66.5 us: gathered(): pl.pallas_call(gather_kernel, out_shape=(shape((width, 3 * HALF), BF16),...]
    psum x1 -> x0, blocking collectives: 59.6 us -> none  [shards(): table_grad = lax.psum(padded, 'fsdp')]
    ppermute x0 -> x12, starting transfers between devices: none -> 27.6 us  [the longest x8 22.9 us: shards(): terms.append(lax.ppermute(og[far], 'fsdp', route))]
    ppermute x0 -> x12, waiting for transfers between devices: none -> 15.5 us  [the longest x4 8.18 us: shards(): table_grad = table_grad + lax.ppermute(table_grad, 'fsdp', route)]
    select_n x4 -> x0, other arithmetic: 10.3 us -> none  [both_halves(): jnp.where(core == 0, jnp.concatenate([own, other], axis=0), jnp.concatena...]
    dynamic_slice x4 -> x0, local copies, waits for them, and re-layouts: 9.23 us -> none  [the longest x2 5.28 us: swap_rows(): lax.dynamic_slice_in_dim(full, (1 - core) * row_count, row_count, 0)]
    pallas_call x2 -> x1, Pallas kernels: 9.54 us -> 5.4 us  [rowwise(): pl.pallas_call(kernel, out_shape=jax.ShapeDtypeStruct(arrays[0].shape, BF...]
  transfers between devices with their start and end apart: 10 -> 14, of which waited for: 4 -> 6; matrix products, arithmetic and copies ran while one was open for 11% -> 3% of each run, Pallas kernels for 12% -> 3%
where the time goes in v2:
time: 192 us
  Pallas kernels  135 us (70%)
  starting transfers between devices  28.1 us (15%)
  waiting for transfers between devices  15.5 us (8%)
  local copies, waits for them, and re-layouts  5.09 us (3%)
  other arithmetic  4.9 us (3%)
  matrix products  2.87 us (1%)
    pallas_call x1, Pallas kernels, gathered(): pl.pallas_call(gather_kernel, out_shape=(shape((width, 3 * HALF), BF16),...  66.5 us
    pallas_call x1, Pallas kernels, shards(): pl.pallas_call(forward_kernel, out_shape=(shape((tokens, 3 * HALF), BF16)...  38.5 us
    pallas_call x1, Pallas kernels, shards(): pl.pallas_call(backward_kernel, out_shape=(shape(fields.shape, BF16), sha...  24.2 us
    ppermute x8, starting transfers between devices, shards(): terms.append(lax.ppermute(og[far], 'fsdp', route))  22.9 us
    ppermute x4, waiting for transfers between devices, shards(): table_grad = table_grad + lax.ppermute(table_grad, 'fsdp', route)  8.18 us
    ppermute x8, waiting for transfers between devices, shards(): terms.append(lax.ppermute(og[far], 'fsdp', route))  7.29 us
    pallas_call x1, Pallas kernels, rowwise(): pl.pallas_call(kernel, out_shape=jax.ShapeDtypeStruct(arrays[0].shape, BF...  5.4 us
    ppermute x4, starting transfers between devices, shards(): table_grad = table_grad + lax.ppermute(table_grad, 'fsdp', route)  4.67 us
  transfers between devices with their start and end apart: 14, of which 6 were waited for; matrix products, arithmetic and copies ran while one was open for 3% of the time, Pallas kernels for 3%

profile of v2, /device:TPU:0, one launch (start us, length us, event | category | flops | bytes accessed | tf_op | source)
XLA Modules:
  0.0 192.0 jit_solution(1848469630110847058)
XLA Ops:
  0.6 0.0 copy-start
  0.7 0.7 copy-done
  1.4 0.1 reshape.50
  1.5 0.3 convolution_bitcast_fusion.2
  1.7 0.9 convolution_bitcast_fusion
  2.6 0.2 copy.10
  2.8 0.0 copy-start.2
  2.8 0.4 tile.10
  3.2 0.3 tile.11
  3.5 1.2 tile.12.bias_ref
  4.7 0.0 copy-done.2
  4.7 0.6 pad_add_fusion.shifts
  5.3 66.5 %shard_map.93 = (bf16[1536,1152]{1,0:T(8,128)(2,1)}, bf16[8,2,48,1536]{3,2,1,0:T(8,128)(2,1)}, bf16[2,16,32,1536]{3,2,1,0:T(8,128)(2,1)}, bf16[2,16,32,1536]{3,2,1,0:T(8,128)(2,1)}) custom-call(bf16[96,2304]{1,0:T(8,128)(2,1)} %w_ref.1, bf16[48,1536]{1,0:T(8,128)(2,1)} %ow_ref.1, bf16[16,32,1536]{2,1,0:T(8,128)(2,1)} %x_ref.3, bf16[16,32,1536]{2,1,0:T(8,128)(2,1)} %cot_ref.1), custom_call_target="tpu_custom_call" | custom-call | flops 100000000 | bytes 100000000 | tf_op jit(solution)/shard_map/pallas_call | solution.py:395
  71.8 38.5 %shard_map.94 = (bf16[1024,1152]{1,0:T(8,128)(2,1)}, f32[48,128,128]{2,1,0:T(8,128)}, bf16[1024,384]{1,0:T(8,128)(2,1)}, bf16[16,32,1536]{2,1,0:T(8,128)(2,1)}, ...) custom-call(s32[4]{0:T(128)} %pad_add_fusion.shifts, bf16[32,32,1536]{2,1,0:T(8,128)(2,1)} %bitcast.59, ...), custom_call_target="tpu_custom_call" | custom-call | flops 10000000000 | bytes 20000000 | tf_op jit(solution)/shard_map/pallas_call | solution.py:461
  110.3 24.2 %shard_map.95 = (bf16[16,32,1536]{2,1,0:T(8,128)(2,1)}, bf16[16,32,1536]{2,1,0:T(8,128)(2,1)}, f32[6,128,128]{2,1,0:T(8,128)}) custom-call(s32[4]{0:T(128)} %pad_add_fusion.shifts, bf16[1024,1152]{1,0:T(8,128)(2,1)} %get-tuple-element.23.packed_ref, f32[48,128,128]{2,1,0:T(8,128)} %get-tuple-element.24.prob_ref, ...), custom_call_target="tpu_custom_call" | custom-call | flops 10000000000 | bytes 20000000 | tf_op jit(solution)/shard_map/pallas_call | solution.py:486
  134.6 0.0 collective-permute-start.1
  134.6 0.5 collective-permute-start
  135.1 1.1 slice_add_fusion
  136.2 0.4 reshape.47
  136.7 1.4 convolution_bitcast_fusion.1
  138.1 0.3 convolution_bitcast_fusion.3
  138.4 0.1 reshape.48
  138.5 0.2 dynamic_update_slice.5
  138.7 0.1 collective-permute-start.10
  138.8 1.4 slice_bitcast_fusion.7
  140.2 0.7 collective-permute-start.2
  140.9 5.9 %collective-permute-start.3 = (bf16[48,1536]{1,0:T(8,128)(2,1)S(1)}, bf16[48,1536]{1,0:T(8,128)(2,1)S(1)}, u32[]{:S(2)}, u32[]{:S(2)}) collective-permute-start(bf16[48,1536]{1,0:T(8,128)(2,1)S(1)} %get-tuple-element.37), channel_id=1, source_target_pairs={{0,1},{1,9},{2,2},{3,10},{4,3},{5,11},{6,4},{7,12},{8,5},{9,13},{1... | collective-permute-start | bytes 442376 | tf_op jit(solution)/shard_map/ppermute | solution.py:483
  146.7 0.0 collective-permute-done.10
  146.8 0.2 add.70
  146.9 0.1 collective-permute-start.11
  147.0 4.0 %collective-permute-done.11 = f32[12,225]{1,0:T(8,128)S(1)} collective-permute-done((f32[12,225]{1,0:T(8,128)S(1)}, f32[12,225]{1,0:T(8,128)S(1)}, u32[]{:S(2)}, u32[]{:S(2)}) %collective-permute-start.11) | collective-permute-done | bytes 10832 | tf_op jit(solution)/shard_map/ppermute | solution.py:516
  151.0 2.4 %collective-permute-start.12 = (f32[12,225]{1,0:T(8,128)S(1)}, f32[12,225]{1,0:T(8,128)S(1)}, u32[]{:S(2)}, u32[]{:S(2)}) collective-permute-start(f32[12,225]{1,0:T(8,128)S(1)} %add.71), channel_id=1, source_target_pairs={{0,4},{1,5},{2,6},{3,7},{4,0},{5,1},{6,2},{7,3},{8,12},{9,13},{10,... | collective-permute-start | bytes 32408 | tf_op jit(solution)/shard_map/ppermute | solution.py:516
  153.4 1.7 collective-permute-done.12
  155.1 2.2 %collective-permute-start.13 = (f32[12,225]{1,0:T(8,128)S(1)}, f32[12,225]{1,0:T(8,128)S(1)}, u32[]{:S(2)}, u32[]{:S(2)}) collective-permute-start(f32[12,225]{1,0:T(8,128)S(1)} %add.72), channel_id=1, source_target_pairs={{0,8},{1,9},{2,10},{3,11},{4,12},{5,13},{6,14},{7,15},{8,0},{9,1},... | collective-permute-start | bytes 32408 | tf_op jit(solution)/shard_map/ppermute | solution.py:516
  157.2 2.5 %collective-permute-done.13 = f32[12,225]{1,0:T(8,128)S(1)} collective-permute-done((f32[12,225]{1,0:T(8,128)S(1)}, f32[12,225]{1,0:T(8,128)S(1)}, u32[]{:S(2)}, u32[]{:S(2)}) %collective-permute-start.13) | collective-permute-done | bytes 10832 | tf_op jit(solution)/shard_map/ppermute | solution.py:516
  159.7 1.9 collective-permute-start.4
  161.6 0.0 collective-permute-done.2
  161.6 1.9 %collective-permute-start.5 = (bf16[48,1536]{1,0:T(8,128)(2,1)S(1)}, bf16[48,1536]{1,0:T(8,128)(2,1)S(1)}, u32[]{:S(2)}, u32[]{:S(2)}) collective-permute-start(bf16[48,1536]{1,0:T(8,128)(2,1)S(1)} %get-tuple-element.35), channel_id=1, source_target_pairs={{0,3},{1,11},{2,4},{3,12},{4,5},{5,13},{6,6},{7,14},{8,7},{9,15},{... | collective-permute-start | bytes 442376 | tf_op jit(solution)/shard_map/ppermute | solution.py:483
  163.6 0.0 collective-permute-done.3
  163.6 3.9 %collective-permute-start.6 = (bf16[48,1536]{1,0:T(8,128)(2,1)S(1)}, bf16[48,1536]{1,0:T(8,128)(2,1)S(1)}, u32[]{:S(2)}, u32[]{:S(2)}) collective-permute-start(bf16[48,1536]{1,0:T(8,128)(2,1)S(1)} %get-tuple-element.34), channel_id=1, source_target_pairs={{0,4},{1,12},{2,5},{3,13},{4,6},{5,14},{6,7},{7,15},{8,0},{9,8},{1... | collective-permute-start | bytes 442376 | tf_op jit(solution)/shard_map/ppermute | solution.py:483
  167.5 2.6 %collective-permute-done.4 = bf16[48,1536]{1,0:T(8,128)(2,1)S(1)} collective-permute-done((bf16[48,1536]{1,0:T(8,128)(2,1)S(1)}, bf16[48,1536]{1,0:T(8,128)(2,1)S(1)}, u32[]{:S(2)}, u32[]{:S(2)}) %collective-permute-start.4) | collective-permute-done | bytes 147488 | tf_op jit(solution)/shard_map/ppermute | solution.py:483
  170.1 1.9 collective-permute-start.7
  172.0 0.0 collective-permute-done.5
  172.0 4.8 %collective-permute-start.8 = (bf16[48,1536]{1,0:T(8,128)(2,1)S(1)}, bf16[48,1536]{1,0:T(8,128)(2,1)S(1)}, u32[]{:S(2)}, u32[]{:S(2)}) collective-permute-start(bf16[48,1536]{1,0:T(8,128)(2,1)S(1)} %get-tuple-element.32), channel_id=1, source_target_pairs={{0,6},{1,14},{2,7},{3,15},{4,0},{5,8},{6,1},{7,9},{8,2},{9,10},{10... | collective-permute-start | bytes 442376 | tf_op jit(solution)/shard_map/ppermute | solution.py:483
  176.8 0.0 collective-permute-done.6
  176.8 1.9 %collective-permute-start.9 = (bf16[48,1536]{1,0:T(8,128)(2,1)S(1)}, bf16[48,1536]{1,0:T(8,128)(2,1)S(1)}, u32[]{:S(2)}, u32[]{:S(2)}) collective-permute-start(bf16[48,1536]{1,0:T(8,128)(2,1)S(1)} %get-tuple-element.31), channel_id=1, source_target_pairs={{0,7},{1,15},{2,0},{3,8},{4,1},{5,9},{6,2},{7,10},{8,3},{9,11},{10... | collective-permute-start | bytes 442376 | tf_op jit(solution)/shard_map/ppermute | solution.py:483
  178.8 0.6 add.73
  179.4 0.0 collective-permute-done.7
  179.4 1.3 collective-permute-done.8
  180.7 3.4 %collective-permute-done.9 = bf16[48,1536]{1,0:T(8,128)(2,1)S(1)} collective-permute-done((bf16[48,1536]{1,0:T(8,128)(2,1)S(1)}, bf16[48,1536]{1,0:T(8,128)(2,1)S(1)}, u32[]{:S(2)}, u32[]{:S(2)}) %collective-permute-start.9) | collective-permute-done | bytes 147488 | tf_op jit(solution)/shard_map/ppermute | solution.py:483
  184.1 0.9 convert_add_fusion
  184.9 0.0 collective-permute-done.1.b_ref
  184.9 0.0 copy-start.1
  184.9 5.4 %shard_map.96 = bf16[16,32,1536]{2,1,0:T(8,128)(2,1)} custom-call(bf16[16,32,1536]{2,1,0:T(8,128)(2,1)} %x_ref.3, bf16[16,32,1536]{2,1,0:T(8,128)(2,1)} %get-tuple-element.26.a_ref, bf16[16,32,1536]{2,1,0:T(8,128)(2,1)} %collective-permute-done.1.b_ref), custom_call_target="tpu_custom_call" | custom-call | flops 15728640 | bytes 4718592 | tf_op jit(solution)/shard_map/pallas_call | solution.py:199
  190.3 0.0 collective-permute-done
  190.3 0.0 copy-done.1
  190.3 1.6 add_convert_fusion
  (6 shorter events, 0.0 us)
Async XLA Ops:
  0.6 0.7 copy-start
  2.8 1.9 %copy-start.2 = (s32[2]{0:T(128)S(1)}, s32[2]{0:T(128)}, u32[]{:S(2)}) copy-start(s32[2]{0:T(128)} %param.7) | copy-start | bytes 28
  134.6 50.3 %collective-permute-start.1 = (bf16[16,32,1536]{2,1,0:T(8,128)(2,1)}, bf16[16,32,1536]{2,1,0:T(8,128)(2,1)}, u32[]{:S(2)}, u32[]{:S(2)}) collective-permute-start(bf16[16,32,1536]{2,1,0:T(8,128)(2,1)} %get-tuple-element.27), channel_id=1, source_target_pairs={{0,1},{1,0},{2,3},{3,2},{4,5},{5,4},{6,7},{7,6},{8,9},{9,8},{10,11... | collective-permute-start | bytes 4718600 | tf_op jit(solution)/shard_map/ppermute | solution.py:30
  134.6 55.7 %collective-permute-start = (bf16[16,32,1536]{2,1,0:T(8,128)(2,1)}, bf16[16,32,1536]{2,1,0:T(8,128)(2,1)S(1)}, u32[]{:S(2)}, u32[]{:S(2)}) collective-permute-start(bf16[16,32,1536]{2,1,0:T(8,128)(2,1)} %get-tuple-element.22), channel_id=1, source_target_pairs={{0,1},{1,0},{2,3},{3,2},{4,5},{5,4},{6,7},{7,6},{8,9},{9,8},{10,11... | collective-permute-start | bytes 4718600 | tf_op jit(solution)/shard_map/ppermute | solution.py:30
  138.7 8.0 %collective-permute-start.10 = (f32[12,225]{1,0:T(8,128)S(1)}, f32[12,225]{1,0:T(8,128)S(1)}, u32[]{:S(2)}, u32[]{:S(2)}) collective-permute-start(f32[12,225]{1,0:T(8,128)S(1)} %dynamic_update_slice.5), channel_id=1, source_target_pairs={{0,1},{1,0},{2,3},{3,2},{4,5},{5,4},{6,7},{7,6},{8,9},{9,8},{10,11... | collective-permute-start | bytes 32408 | tf_op jit(solution)/shard_map/ppermute | solution.py:516
  140.2 21.4 %collective-permute-start.2 = (bf16[48,1536]{1,0:T(8,128)(2,1)S(1)}, bf16[48,1536]{1,0:T(8,128)(2,1)S(1)}, u32[]{:S(2)}, u32[]{:S(2)}) collective-permute-start(bf16[48,1536]{1,0:T(8,128)(2,1)S(1)} %get-tuple-element.30), channel_id=1, source_target_pairs={{0,0},{1,8},{2,1},{3,9},{4,2},{5,10},{6,3},{7,11},{8,4},{9,12},{10... | collective-permute-start | bytes 442376 | tf_op jit(solution)/shard_map/ppermute | solution.py:483
  140.9 22.7 %collective-permute-start.3 = (bf16[48,1536]{1,0:T(8,128)(2,1)S(1)}, bf16[48,1536]{1,0:T(8,128)(2,1)S(1)}, u32[]{:S(2)}, u32[]{:S(2)}) collective-permute-start(bf16[48,1536]{1,0:T(8,128)(2,1)S(1)} %get-tuple-element.37), channel_id=1, source_target_pairs={{0,1},{1,9},{2,2},{3,10},{4,3},{5,11},{6,4},{7,12},{8,5},{9,13},{1... | collective-permute-start | bytes 442376 | tf_op jit(solution)/shard_map/ppermute | solution.py:483
  146.9 4.1 %collective-permute-start.11 = (f32[12,225]{1,0:T(8,128)S(1)}, f32[12,225]{1,0:T(8,128)S(1)}, u32[]{:S(2)}, u32[]{:S(2)}) collective-permute-start(f32[12,225]{1,0:T(8,128)S(1)} %add.70), channel_id=1, source_target_pairs={{0,2},{1,3},{2,0},{3,1},{4,6},{5,7},{6,4},{7,5},{8,10},{9,11},{10,... | collective-permute-start | bytes 32408 | tf_op jit(solution)/shard_map/ppermute | solution.py:516
  151.0 4.1 %collective-permute-start.12 = (f32[12,225]{1,0:T(8,128)S(1)}, f32[12,225]{1,0:T(8,128)S(1)}, u32[]{:S(2)}, u32[]{:S(2)}) collective-permute-start(f32[12,225]{1,0:T(8,128)S(1)} %add.71), channel_id=1, source_target_pairs={{0,4},{1,5},{2,6},{3,7},{4,0},{5,1},{6,2},{7,3},{8,12},{9,13},{10,... | collective-permute-start | bytes 32408 | tf_op jit(solution)/shard_map/ppermute | solution.py:516
  155.1 4.6 %collective-permute-start.13 = (f32[12,225]{1,0:T(8,128)S(1)}, f32[12,225]{1,0:T(8,128)S(1)}, u32[]{:S(2)}, u32[]{:S(2)}) collective-permute-start(f32[12,225]{1,0:T(8,128)S(1)} %add.72), channel_id=1, source_target_pairs={{0,8},{1,9},{2,10},{3,11},{4,12},{5,13},{6,14},{7,15},{8,0},{9,1},... | collective-permute-start | bytes 32408 | tf_op jit(solution)/shard_map/ppermute | solution.py:516
  159.7 10.4 %collective-permute-start.4 = (bf16[48,1536]{1,0:T(8,128)(2,1)S(1)}, bf16[48,1536]{1,0:T(8,128)(2,1)S(1)}, u32[]{:S(2)}, u32[]{:S(2)}) collective-permute-start(bf16[48,1536]{1,0:T(8,128)(2,1)S(1)} %get-tuple-element.36), channel_id=1, source_target_pairs={{0,2},{1,10},{2,3},{3,11},{4,4},{5,12},{6,5},{7,13},{8,6},{9,14},{... | collective-permute-start | bytes 442376 | tf_op jit(solution)/shard_map/ppermute | solution.py:483
  161.6 10.3 %collective-permute-start.5 = (bf16[48,1536]{1,0:T(8,128)(2,1)S(1)}, bf16[48,1536]{1,0:T(8,128)(2,1)S(1)}, u32[]{:S(2)}, u32[]{:S(2)}) collective-permute-start(bf16[48,1536]{1,0:T(8,128)(2,1)S(1)} %get-tuple-element.35), channel_id=1, source_target_pairs={{0,3},{1,11},{2,4},{3,12},{4,5},{5,13},{6,6},{7,14},{8,7},{9,15},{... | collective-permute-start | bytes 442376 | tf_op jit(solution)/shard_map/ppermute | solution.py:483
  163.6 13.2 %collective-permute-start.6 = (bf16[48,1536]{1,0:T(8,128)(2,1)S(1)}, bf16[48,1536]{1,0:T(8,128)(2,1)S(1)}, u32[]{:S(2)}, u32[]{:S(2)}) collective-permute-start(bf16[48,1536]{1,0:T(8,128)(2,1)S(1)} %get-tuple-element.34), channel_id=1, source_target_pairs={{0,4},{1,12},{2,5},{3,13},{4,6},{5,14},{6,7},{7,15},{8,0},{9,8},{1... | collective-permute-start | bytes 442376 | tf_op jit(solution)/shard_map/ppermute | solution.py:483
  170.1 9.3 %collective-permute-start.7 = (bf16[48,1536]{1,0:T(8,128)(2,1)S(1)}, bf16[48,1536]{1,0:T(8,128)(2,1)S(1)}, u32[]{:S(2)}, u32[]{:S(2)}) collective-permute-start(bf16[48,1536]{1,0:T(8,128)(2,1)S(1)} %get-tuple-element.33), channel_id=1, source_target_pairs={{0,5},{1,13},{2,6},{3,14},{4,7},{5,15},{6,0},{7,8},{8,1},{9,9},{10... | collective-permute-start | bytes 442376 | tf_op jit(solution)/shard_map/ppermute | solution.py:483
  172.0 8.7 %collective-permute-start.8 = (bf16[48,1536]{1,0:T(8,128)(2,1)S(1)}, bf16[48,1536]{1,0:T(8,128)(2,1)S(1)}, u32[]{:S(2)}, u32[]{:S(2)}) collective-permute-start(bf16[48,1536]{1,0:T(8,128)(2,1)S(1)} %get-tuple-element.32), channel_id=1, source_target_pairs={{0,6},{1,14},{2,7},{3,15},{4,0},{5,8},{6,1},{7,9},{8,2},{9,10},{10... | collective-permute-start | bytes 442376 | tf_op jit(solution)/shard_map/ppermute | solution.py:483
  176.8 7.2 %collective-permute-start.9 = (bf16[48,1536]{1,0:T(8,128)(2,1)S(1)}, bf16[48,1536]{1,0:T(8,128)(2,1)S(1)}, u32[]{:S(2)}, u32[]{:S(2)}) collective-permute-start(bf16[48,1536]{1,0:T(8,128)(2,1)S(1)} %get-tuple-element.31), channel_id=1, source_target_pairs={{0,7},{1,15},{2,0},{3,8},{4,1},{5,9},{6,2},{7,10},{8,3},{9,11},{10... | collective-permute-start | bytes 442376 | tf_op jit(solution)/shard_map/ppermute | solution.py:483
  184.9 5.4 %copy-start.1 = (bf16[16,32,1536]{2,1,0:T(8,128)(2,1)S(1)}, bf16[16,32,1536]{2,1,0:T(8,128)(2,1)}, u32[]{:S(2)}) copy-start(bf16[16,32,1536]{2,1,0:T(8,128)(2,1)} %get-tuple-element.21) | copy-start | bytes 4718596

commit v3 on v2

--- a/solution.py
+++ b/solution.py
@@ -168,6 +168,146 @@
         dsh = dot(dpk[...], w_ref[...], ((1,), (1,))).astype(BF16)
         back = dot(perm, dsh, ((0,), (0,))).astype(BF16)
         write_band(own_ref, give_ref, back, band, shift_h, shifts[2])
+        return 0
+
+    lax.fori_loop(0, BANDS, body, 0)
+
+
+def joint_kernel(
+    shifts, packed_ref, prob_ref, dctx_ref, w_ref, og_ref, give_ref,
+    down_ref, dgot_ref, agot_ref, out_ref, score_ref,
+    dpk, table, first, second, slots, sums, seen,
+    part_send, part_recv, local, tok_send, tok_recv, cube_send, cube_recv,
+):
+    me = lax.axis_index("fsdp")
+    core = me % 2
+    chip = me // 2
+    count = 16
+    other = chip * 2 + (1 - core)
+    barrier = pltpu.get_barrier_semaphore()
+    for far in range(1, count):
+        pl.semaphore_signal(
+            barrier, inc=1, device_id={"fsdp": (me + far) % count}, device_id_type=MESH
+        )
+    pl.semaphore_wait(barrier, count - 1)
+
+    def remote(src, dst, send, recv, target):
+        return pltpu.make_async_remote_copy(
+            src_ref=src, dst_ref=dst, send_sem=send, recv_sem=recv,
+            device_id={"fsdp": target}, device_id_type=MESH,
+        )
+
+    a_copy = remote(give_ref, agot_ref, tok_send.at[0], tok_recv.at[0], other)
+    a_copy.start()
+    dests = [core * 8 + (chip + far) % 8 for far in range(8)]
+
+    def part(far):
+        return remote(
+            og_ref.at[far], slots.at[far], part_send.at[far], part_recv.at[far], dests[far]
+        )
+
+    def near(far):
+        return pltpu.make_async_copy(og_ref.at[far], slots.at[far], local.at[far])
+
+    for far in range(8):
+
+        @pl.when(dests[far] != me)
+        def _():
+            part(far).start()
+
+        @pl.when(dests[far] == me)
+        def _():
+            near(far).start()
+
+    backward_bands(shifts, packed_ref, prob_ref, dctx_ref, w_ref, first, table, dpk)
+
+    sums[0] = table[:, :64, :64] + table[:, 64:, 64:]
+
+    def cube(step):
+        peer = chip + (1 << step) * (1 - 2 * ((chip // (1 << step)) % 2))
+        return remote(
+            sums.at[step], seen.at[step], cube_send.at[step], cube_recv.at[step], peer * 2 + core
+        )
+
+    src, dst = first, second
+    for step in range(3):
+        cube(step).start()
+        taken = (shifts[0] >> step) & 1
+        back = 1 << step
+
+        def roll(row, _):
+            dst[row] = jnp.where(taken == 1, src[lax.rem(row + SIDE - back, SIDE)], src[row])
+            return 0
+
+        lax.fori_loop(0, SIDE, roll, 0)
+        src, dst = dst, src
+        if step == 2:
+            half = SIDE // 2
+            d_copy = remote(
+                src.at[pl.ds((1 - core) * half, half)], dgot_ref, tok_send.at[1], tok_recv.at[1], other
+            )
+            d_copy.start()
+        cube(step).wait()
+        sums[step + 1] = sums[step] + seen[step]
+    last = remote(sums.at[3], seen.at[3], cube_send.at[3], cube_recv.at[3], other)
+    last.start()
+
+    def keep(row, _):
+        down_ref[row] = src[core * (SIDE // 2) + row]
+        return 0
+
+    lax.fori_loop(0, SIDE // 2, keep, 0)
+    for far in range(8):
+
+        @pl.when(dests[far] != me)
+        def _():
+            part(far).wait()
+
+        @pl.when(dests[far] == me)
+        def _():
+            near(far).wait()
+
+    total = slots[0].astype(F32)
+    for far in range(1, 8):
+        total = total + slots[far].astype(F32)
+    out_ref[...] = total
+    last.wait()
+    score_ref[core] = sums[3]
+    score_ref[1 - core] = seen[3]
+    a_copy.wait()
+    d_copy.wait()
+
+
+def backward_bands(shifts, packed_ref, prob_ref, dctx_ref, w_ref, out_ref, table_ref, dpk):
+    shift_w = shifts[1]
+    perm = band_permutation(shift_w)
+    scale = HD**-0.5
+    table_ref[...] = jnp.zeros_like(table_ref)
+
+    def body(band, _):
+        for pair in range(2):
+            rows = pl.ds(pl.multiple_of(band * BAND + pair * PAIR, PAIR), PAIR)
+            packed = packed_ref[rows, :]
+            dctx = dctx_ref[rows, :]
+            dqs, dks, dvs = [], [], []
+            for h in range(MINE):
+                q = packed[:, h * HD : (h + 1) * HD]
+                k = packed[:, HALF + h * HD : HALF + (h + 1) * HD]
+                v = packed[:, 2 * HALF + h * HD : 2 * HALF + (h + 1) * HD]
+                d = dctx[:, h * HD : (h + 1) * HD]
+                p = prob_ref[(band * 2 + pair) * MINE + h]
+                dp = dot(d, v, ((1,), (1,)))
+                dvs.append(dot(p.astype(BF16), d, ((0,), (0,))).astype(BF16))
+                ds = p * (dp - jnp.sum(p * dp, axis=-1, keepdims=True))
+                table_ref[h] += ds
+                low = ds.astype(BF16)
+                dqs.append((dot(low, k) * scale).astype(BF16))
+                dks.append((dot(low, q, ((0,), (0,))) * scale).astype(BF16))
+            dpk[pair * PAIR : (pair + 1) * PAIR, :] = jnp.concatenate(dqs + dks + dvs, axis=1)
+        dsh = dot(dpk[...], w_ref[...], ((1,), (1,))).astype(BF16)
+        back = dot(perm, dsh, ((0,), (0,))).astype(BF16)
+        for i in range(WIN):
+            out_ref[band * WIN + i] = back[i * SIDE : (i + 1) * SIDE]
         return 0
 
     lax.fori_loop(0, BANDS, body, 0)
@@ -414,6 +554,37 @@
     )(in_weight, out_weight, fields, cotangent)
 
 
+def joint_call(scalars, packed, prob, dctx, w_full, og, give):
+    dma = pltpu.SemaphoreType.DMA
+    area = WIN * WIN
+    return pl.pallas_call(
+        joint_kernel,
+        out_shape=(
+            shape(give.shape, BF16),
+            shape(give.shape, BF16),
+            shape(give.shape, BF16),
+            shape(og.shape[1:], F32),
+            shape((2, MINE, area, area), F32),
+        ),
+        in_specs=[pl.BlockSpec(memory_space=pltpu.SMEM)] + whole(6),
+        out_specs=tuple(whole(5)),
+        scratch_shapes=[
+            pltpu.VMEM((BAND, 3 * HALF), BF16),
+            pltpu.VMEM((MINE, PAIR, PAIR), F32),
+            pltpu.VMEM((SIDE, SIDE, give.shape[2]), BF16),
+            pltpu.VMEM((SIDE, SIDE, give.shape[2]), BF16),
+            pltpu.VMEM(og.shape, BF16),
+            pltpu.VMEM((4, MINE, area, area), F32),
+            pltpu.VMEM((4, MINE, area, area), F32),
+            dma((8,)), dma((8,)), dma((8,)), dma((2,)), dma((2,)), dma((4,)), dma((4,)),
+        ],
+        compiler_params=pltpu.CompilerParams(
+            collective_id=1, has_side_effects=True, vmem_limit_bytes=VMEM_LIMIT
+        ),
+        cost_estimate=pl.CostEstimate(flops=10**10, bytes_accessed=2 * 10**7, transcendentals=0),
+    )(scalars, packed, prob, dctx, w_full, og, give)
+
+
 def gathered_plain(fields, in_weight, out_weight, cotangent):
     core = lax.axis_index("fsdp") % 2
     groups = same_core_groups()
@@ -475,12 +646,24 @@
         cost_estimate=pl.CostEstimate(flops=10**10, bytes_accessed=2 * 10**7, transcendentals=10**6),
     )(scalars, x_all, cot_all, w_full, ow_full, bias)
 
+    joint = 2 * chips == 16
     terms = []
-    for far in range(chips):
+    for far in range(0 if joint else chips):
         route = [
             (2 * c + k, k * chips + (c + far) % chips) for c in range(chips) for k in range(2)
         ]
         terms.append(lax.ppermute(og[far], "fsdp", route))
+    if joint:
+        d_own, d_got, a_got, out_grad, score = joint_call(
+            scalars, packed, prob, dctx, w_full, og, a_give
+        )
+        attended = (a_own.astype(F32) + a_got.astype(F32)).astype(BF16)
+        fields_gradient = rowwise(norm_back_kernel, fields, d_own, d_got)
+        local = score.reshape(HEADS, WIN, WIN, WIN, WIN)
+        table_grad = jnp.einsum(
+            "hprqs,pqu,rsv->huv", local, table, table, precision=lax.Precision.HIGHEST
+        ).reshape(HEADS, span * span)
+        return (attended, fields_gradient, out_grad, table_grad)
     a_got = partner(a_give)
 
     d_own, d_give, score = pl.pallas_call(

time: 192 us -> 183 us (0.953)
  Pallas kernels: 135 us -> 168 us
  starting transfers between devices: 28.1 us -> 0 us
  waiting for transfers between devices: 15.5 us -> 0 us
  matrix products: 2.87 us -> 5.02 us
    pallas_call x1, Pallas kernels: 24.2 us -> 57.7 us  [joint_call(): pl.pallas_call(joint_kernel, out_shape=(shape(give.shape, BF16), shape(gi...]
    ppermute x14 -> x0, starting transfers between devices: 28.1 us -> none  [the longest x8 22.9 us: shards(): terms.append(lax.ppermute(og[far], 'fsdp', route))]
    ppermute x14 -> x0, waiting for transfers between devices: 15.5 us -> none  [the longest x4 8.18 us: shards(): table_grad = table_grad + lax.ppermute(table_grad, 'fsdp', route)]
    add x5 -> x0, other arithmetic: 2.62 us -> none  [the longest x1 1.14 us: shards(): score[:, :area, :area] + score[:, area:, area:]]
    dot_general x2, matrix products: 1.74 us -> 3.89 us  [shards(): jnp.einsum('hprqs,pqu,rsv->huv', local, table, table, precision=lax.Preci...]
  transfers between devices with their start and end apart: 14 -> 0, of which waited for: 6 -> 0; matrix products, arithmetic and copies ran while one was open for 3% -> 0% of each run, Pallas kernels for 3% -> 0%
where the time goes in v3:
time: 183 us
  Pallas kernels  168 us (92%)
  matrix products  5.02 us (3%)
  local copies, waits for them, and re-layouts  4.69 us (3%)
  other arithmetic  4.27 us (2%)
    pallas_call x1, Pallas kernels, gathered(): pl.pallas_call(gather_kernel, out_shape=(shape((width, 3 * HALF), BF16),...  66.5 us
    pallas_call x1, Pallas kernels, joint_call(): pl.pallas_call(joint_kernel, out_shape=(shape(give.shape, BF16), shape(gi...  57.7 us
    pallas_call x1, Pallas kernels, shards(): pl.pallas_call(forward_kernel, out_shape=(shape((tokens, 3 * HALF), BF16)...  38.5 us
    pallas_call x1, Pallas kernels, rowwise(): pl.pallas_call(kernel, out_shape=jax.ShapeDtypeStruct(arrays[0].shape, BF...  5.32 us
    dot_general x2, matrix products, shards(): jnp.einsum('hprqs,pqu,rsv->huv', local, table, table, precision=lax.Preci...  3.89 us

profile of v3, /device:TPU:0, one launch (start us, length us, event | category | flops | bytes accessed | tf_op | source)
XLA Modules:
  0.0 182.7 jit_solution(16355523636921938599)
XLA Ops:
  0.6 0.0 copy-start
  0.7 1.2 pad_add_fusion.shifts
  1.9 0.0 copy-done
  1.9 0.0 copy-start.4
  1.9 0.1 reshape.50
  2.0 0.3 convolution_bitcast_fusion.2
  2.3 0.2 copy-done.4
  2.5 0.9 convolution_bitcast_fusion
  3.4 0.1 copy.10
  3.5 0.4 tile.10
  3.9 0.3 tile.11
  4.2 1.2 tile.12.bias_ref
  5.4 66.5 %shard_map.93 = (bf16[1536,1152]{1,0:T(8,128)(2,1)}, bf16[8,2,48,1536]{3,2,1,0:T(8,128)(2,1)}, bf16[2,16,32,1536]{3,2,1,0:T(8,128)(2,1)}, bf16[2,16,32,1536]{3,2,1,0:T(8,128)(2,1)}) custom-call(bf16[96,2304]{1,0:T(8,128)(2,1)} %w_ref.1, bf16[48,1536]{1,0:T(8,128)(2,1)} %ow_ref.1, bf16[16,32,1536]{2,1,0:T(8,128)(2,1)} %x_ref.3, bf16[16,32,1536]{2,1,0:T(8,128)(2,1)} %cot_ref.1), custom_call_target="tpu_custom_call" | custom-call | flops 100000000 | bytes 100000000 | tf_op jit(solution)/shard_map/pallas_call | solution.py:535
  71.9 38.5 %shard_map.94 = (bf16[1024,1152]{1,0:T(8,128)(2,1)}, f32[48,128,128]{2,1,0:T(8,128)}, bf16[1024,384]{1,0:T(8,128)(2,1)}, bf16[16,32,1536]{2,1,0:T(8,128)(2,1)}, ...) custom-call(s32[4]{0:T(128)} %pad_add_fusion.shifts, bf16[32,32,1536]{2,1,0:T(8,128)(2,1)} %bitcast.45, ...), custom_call_target="tpu_custom_call" | custom-call | flops 10000000000 | bytes 20000000 | tf_op jit(solution)/shard_map/pallas_call | solution.py:632
  110.4 0.0 copy-start.1
  110.4 57.7 %shard_map.95 = (bf16[16,32,1536]{2,1,0:T(8,128)(2,1)}, bf16[16,32,1536]{2,1,0:T(8,128)(2,1)}, bf16[16,32,1536]{2,1,0:T(8,128)(2,1)}, f32[48,1536]{1,0:T(8,128)}, f32[2,6,64,64]{3,2,1,0:T(8,128)}) custom-call(s32[4]{0:T(128)} %pad_add_fusion.shifts, bf16[1024,1152]{1,0:T(8,128)(2,1)} %get-tuple-element.24.packed_ref, ...), custom_call_target="tpu_custom_call" | custom-call | flops 10000000000 | bytes 20000000 | tf_op jit(solution)/shard_map/pallas_call | solution.py:560
  168.1 0.0 copy-done.1
  168.1 3.0 %add_convert_fusion = bf16[16,32,1536]{2,1,0:T(8,128)(2,1)} fusion(bf16[16,32,1536]{2,1,0:T(8,128)(2,1)} %get-tuple-element.29, bf16[16,32,1536]{2,1,0:T(8,128)(2,1)S(1)} %copy-done.1), kind=kLoop, calls=%fused_computation | loop fusion | flops 3145728 | bytes 4718592 | tf_op jit(solution)/shard_map/convert_element_type | solution.py:660
  171.1 0.0 copy-start.2
  171.1 5.3 %shard_map.96 = bf16[16,32,1536]{2,1,0:T(8,128)(2,1)} custom-call(bf16[16,32,1536]{2,1,0:T(8,128)(2,1)} %x_ref.3, bf16[16,32,1536]{2,1,0:T(8,128)(2,1)} %get-tuple-element.30.a_ref, bf16[16,32,1536]{2,1,0:T(8,128)(2,1)} %get-tuple-element.31.b_ref), custom_call_target="tpu_custom_call" | custom-call | flops 15728640 | bytes 4718592 | tf_op jit(solution)/shard_map/pallas_call | solution.py:339
  176.4 0.0 copy-done.2
  176.5 0.9 reshape.47
  177.4 0.0 copy-start.5
  177.4 0.0 copy-start.3
  177.4 3.4 %convolution_bitcast_fusion.1 = f32[15,12,8,8]{0,3,2,1:T(8,128)S(1)} fusion(f32[12,8,8,8,8]{4,3,2,1,0:T(8,128)S(1)} %reshape.47, s32[8,8]{1,0:T(8,128)} %copy-done.4), kind=kOutput, calls=%fused_computation.2 | convolution fusion | flops 8848320 | bytes 242944 | tf_op jit(solution)/shard_map/hprqs,pqu,rsv->huv/dot_general | solution.py:663
  180.8 0.0 copy-done.5
  180.8 0.5 convolution_bitcast_fusion.3
  181.3 0.7 reshape.48
  182.0 0.0 copy-done.3
  182.0 0.7 copy.18
  (2 shorter events, 0.0 us)
Async XLA Ops:
  0.6 1.3 copy-start
  1.9 0.6 copy-start.4
  110.4 57.7 %copy-start.1 = (bf16[16,32,1536]{2,1,0:T(8,128)(2,1)S(1)}, bf16[16,32,1536]{2,1,0:T(8,128)(2,1)}, u32[]{:S(2)}) copy-start(bf16[16,32,1536]{2,1,0:T(8,128)(2,1)} %get-tuple-element.23) | copy-start | bytes 4718596
  171.1 5.3 %copy-start.2 = (f32[2,6,64,64]{3,2,1,0:T(8,128)S(1)}, f32[2,6,64,64]{3,2,1,0:T(8,128)}, u32[]{:S(2)}) copy-start(f32[2,6,64,64]{3,2,1,0:T(8,128)} %get-tuple-element.33) | copy-start | bytes 589828
  177.4 3.4 %copy-start.5 = (s32[8,8]{1,0:T(8,128)S(1)}, s32[8,8]{1,0:T(8,128)}, u32[]{:S(2)}) copy-start(s32[8,8]{1,0:T(8,128)} %copy-done.4) | copy-start | bytes 772
  177.4 4.6 %copy-start.3 = (f32[48,1536]{1,0:T(8,128)S(1)}, f32[48,1536]{1,0:T(8,128)}, u32[]{:S(2)}) copy-start(f32[48,1536]{1,0:T(8,128)} %get-tuple-element.40) | copy-start | bytes 884740

commit v4 on v3

--- a/solution.py
+++ b/solution.py
@@ -176,8 +176,8 @@
 def joint_kernel(
     shifts, packed_ref, prob_ref, dctx_ref, w_ref, og_ref, give_ref,
     down_ref, dgot_ref, agot_ref, out_ref, score_ref,
-    dpk, table, first, second, slots, sums, seen,
-    part_send, part_recv, local, tok_send, tok_recv, cube_send, cube_recv,
+    dpk, table, first, second, held, sent, slots, sums, seen,
+    part_send, part_recv, local, ring_send, ring_recv, tok_send, tok_recv, cube_send, cube_recv,
 ):
     me = lax.axis_index("fsdp")
     core = me % 2
@@ -199,27 +199,42 @@
 
     a_copy = remote(give_ref, agot_ref, tok_send.at[0], tok_recv.at[0], other)
     a_copy.start()
-    dests = [core * 8 + (chip + far) % 8 for far in range(8)]
-
-    def part(far):
+    quarter = pl.ds(core * 4, 4)
+    near = pltpu.make_async_copy(og_ref.at[:, core], held.at[quarter], local)
+    far = remote(og_ref.at[:, 1 - core], held.at[quarter], part_send, part_recv, other)
+    near.start()
+    far.start()
+    near.wait()
+    far.wait()
+    place = ring_place(chip)
+    sides = (ring_chip(place + 1) * 2 + core, ring_chip(place - 1) * 2 + core)
+
+    def hop(way, step):
         return remote(
-            og_ref.at[far], slots.at[far], part_send.at[far], part_recv.at[far], dests[far]
-        )
-
-    def near(far):
-        return pltpu.make_async_copy(og_ref.at[far], slots.at[far], local.at[far])
-
-    for far in range(8):
-
-        @pl.when(dests[far] != me)
-        def _():
-            part(far).start()
-
-        @pl.when(dests[far] == me)
-        def _():
-            near(far).start()
-
-    backward_bands(shifts, packed_ref, prob_ref, dctx_ref, w_ref, first, table, dpk)
+            sent.at[way, step], slots.at[way, step], ring_send.at[way, step],
+            ring_recv.at[way, step], sides[way],
+        )
+
+    def travel(step):
+        for way in range(2):
+            owner = ring_chip(place + (4 - step) * (1 - 2 * way))
+
+            @pl.when(step > way)
+            def _():
+                hop(way, step - 1).wait_recv()
+                sent[way, step] = (
+                    held[owner].astype(F32) + slots[way, step - 1].astype(F32)
+                ).astype(BF16)
+
+            @pl.when(step == way)
+            def _():
+                sent[way, step] = held[owner]
+
+            @pl.when(step >= way)
+            def _():
+                hop(way, step).start()
+
+    backward_bands(shifts, packed_ref, prob_ref, dctx_ref, w_ref, first, table, dpk, travel)
 
     sums[0] = table[:, :64, :64] + table[:, 64:, 64:]
 
@@ -257,20 +272,11 @@
         return 0
 
     lax.fori_loop(0, SIDE // 2, keep, 0)
-    for far in range(8):
-
-        @pl.when(dests[far] != me)
-        def _():
-            part(far).wait()
-
-        @pl.when(dests[far] == me)
-        def _():
-            near(far).wait()
-
-    total = slots[0].astype(F32)
-    for far in range(1, 8):
-        total = total + slots[far].astype(F32)
-    out_ref[...] = total
+    for way in range(2):
+        hop(way, 3).wait_recv()
+        for step in range(way, 4):
+            hop(way, step).wait_send()
+    out_ref[...] = held[chip].astype(F32) + slots[0, 3].astype(F32) + slots[1, 3].astype(F32)
     last.wait()
     score_ref[core] = sums[3]
     score_ref[1 - core] = seen[3]
@@ -278,13 +284,14 @@
     d_copy.wait()
 
 
-def backward_bands(shifts, packed_ref, prob_ref, dctx_ref, w_ref, out_ref, table_ref, dpk):
+def backward_bands(shifts, packed_ref, prob_ref, dctx_ref, w_ref, out_ref, table_ref, dpk, travel):
     shift_w = shifts[1]
     perm = band_permutation(shift_w)
     scale = HD**-0.5
     table_ref[...] = jnp.zeros_like(table_ref)
 
     def body(band, _):
+        travel(band)
         for pair in range(2):
             rows = pl.ds(pl.multiple_of(band * BAND + pair * PAIR, PAIR), PAIR)
             packed = packed_ref[rows, :]
@@ -573,16 +580,18 @@
             pltpu.VMEM((MINE, PAIR, PAIR), F32),
             pltpu.VMEM((SIDE, SIDE, give.shape[2]), BF16),
             pltpu.VMEM((SIDE, SIDE, give.shape[2]), BF16),
-            pltpu.VMEM(og.shape, BF16),
+            pltpu.VMEM((8,) + og.shape[1:], BF16),
+            pltpu.VMEM((2, 4) + og.shape[1:], BF16),
+            pltpu.VMEM((2, 4) + og.shape[1:], BF16),
             pltpu.VMEM((4, MINE, area, area), F32),
             pltpu.VMEM((4, MINE, area, area), F32),
-            dma((8,)), dma((8,)), dma((8,)), dma((2,)), dma((2,)), dma((4,)), dma((4,)),
+            dma, dma, dma, dma((2, 4)), dma((2, 4)), dma((2,)), dma((2,)), dma((4,)), dma((4,)),
         ],
         compiler_params=pltpu.CompilerParams(
             collective_id=1, has_side_effects=True, vmem_limit_bytes=VMEM_LIMIT
         ),
         cost_estimate=pl.CostEstimate(flops=10**10, bytes_accessed=2 * 10**7, transcendentals=0),
-    )(scalars, packed, prob, dctx, w_full, og, give)
+    )(scalars, packed, prob, dctx, w_full, og.reshape((4, 2) + og.shape[1:]), give)
 
 
 def gathered_plain(fields, in_weight, out_weight, cotangent):
@@ -612,7 +621,9 @@
     ow_full = ow_all.reshape(2 * HALF, width)
     x_all = x_all.reshape(SIDE, col_count, width)
     cot_all = cot_all.reshape(SIDE, col_count, width)
-    scalars = jnp.concatenate([shifts, jnp.stack([core, lax.axis_index("fsdp") // 2])]).astype(jnp.int32)
+    joint = 2 * chips == 16
+    turn = 0 * core if joint else lax.axis_index("fsdp") // 2
+    scalars = jnp.concatenate([shifts, jnp.stack([core, turn])]).astype(jnp.int32)
 
     table = offset_table(WIN)
     own_table = lax.dynamic_slice_in_dim(bias_table, core * MINE, MINE, 0)
@@ -646,7 +657,6 @@
         cost_estimate=pl.CostEstimate(flops=10**10, bytes_accessed=2 * 10**7, transcendentals=10**6),
     )(scalars, x_all, cot_all, w_full, ow_full, bias)
 
-    joint = 2 * chips == 16
     terms = []
     for far in range(0 if joint else chips):
         route = [

time: 183 us -> 179 us (0.978)
  Pallas kernels: 168 us -> 164 us
    pallas_call x1, Pallas kernels: 57.7 us -> 54 us  [joint_call(): pl.pallas_call(joint_kernel, out_shape=(shape(give.shape, BF16), shape(gi...]
where the time goes in v4:
time: 179 us
  Pallas kernels  164 us (92%)
  matrix products  5.02 us (3%)
  local copies, waits for them, and re-layouts  4.69 us (3%)
  other arithmetic  4.27 us (2%)
    pallas_call x1, Pallas kernels, gathered(): pl.pallas_call(gather_kernel, out_shape=(shape((width, 3 * HALF), BF16),...  66.5 us
    pallas_call x1, Pallas kernels, joint_call(): pl.pallas_call(joint_kernel, out_shape=(shape(give.shape, BF16), shape(gi...  54 us
    pallas_call x1, Pallas kernels, shards(): pl.pallas_call(forward_kernel, out_shape=(shape((tokens, 3 * HALF), BF16)...  38.5 us
    pallas_call x1, Pallas kernels, rowwise(): pl.pallas_call(kernel, out_shape=jax.ShapeDtypeStruct(arrays[0].shape, BF...  5.32 us
    dot_general x2, matrix products, shards(): jnp.einsum('hprqs,pqu,rsv->huv', local, table, table, precision=lax.Preci...  3.89 us

profile of v4, /device:TPU:0, one launch (start us, length us, event | category | flops | bytes accessed | tf_op | source)
XLA Modules:
  0.0 179.0 jit_solution(1534733710395061848)
XLA Ops:
  0.6 0.0 copy-start
  0.7 1.2 pad_add_fusion.shifts
  1.9 0.0 copy-done
  1.9 0.0 copy-start.4
  1.9 0.1 reshape.54
  2.0 0.3 convolution_bitcast_fusion.2
  2.3 0.2 copy-done.4
  2.5 0.9 convolution_bitcast_fusion
  3.4 0.1 copy.10
  3.5 0.4 tile.10
  3.9 0.3 tile.11
  4.2 1.2 tile.12.bias_ref
  5.4 66.5 %shard_map.93 = (bf16[1536,1152]{1,0:T(8,128)(2,1)}, bf16[8,2,48,1536]{3,2,1,0:T(8,128)(2,1)}, bf16[2,16,32,1536]{3,2,1,0:T(8,128)(2,1)}, bf16[2,16,32,1536]{3,2,1,0:T(8,128)(2,1)}) custom-call(bf16[96,2304]{1,0:T(8,128)(2,1)} %w_ref.1, bf16[48,1536]{1,0:T(8,128)(2,1)} %ow_ref.1, bf16[16,32,1536]{2,1,0:T(8,128)(2,1)} %x_ref.3, bf16[16,32,1536]{2,1,0:T(8,128)(2,1)} %cot_ref.1), custom_call_target="tpu_custom_call" | custom-call | flops 100000000 | bytes 100000000 | tf_op jit(solution)/shard_map/pallas_call | solution.py:542
  71.9 38.5 %shard_map.94 = (bf16[1024,1152]{1,0:T(8,128)(2,1)}, f32[48,128,128]{2,1,0:T(8,128)}, bf16[1024,384]{1,0:T(8,128)(2,1)}, bf16[16,32,1536]{2,1,0:T(8,128)(2,1)}, ...) custom-call(s32[4]{0:T(128)} %pad_add_fusion.shifts, bf16[32,32,1536]{2,1,0:T(8,128)(2,1)} %bitcast.45, ...), custom_call_target="tpu_custom_call" | custom-call | flops 10000000000 | bytes 20000000 | tf_op jit(solution)/shard_map/pallas_call | solution.py:643
  110.4 0.0 copy-start.1
  110.4 54.0 %shard_map.95 = (bf16[16,32,1536]{2,1,0:T(8,128)(2,1)}, bf16[16,32,1536]{2,1,0:T(8,128)(2,1)}, bf16[16,32,1536]{2,1,0:T(8,128)(2,1)}, f32[48,1536]{1,0:T(8,128)}, f32[2,6,64,64]{3,2,1,0:T(8,128)}) custom-call(s32[4]{0:T(128)} %pad_add_fusion.shifts, bf16[1024,1152]{1,0:T(8,128)(2,1)} %get-tuple-element.24.packed_ref, ...), custom_call_target="tpu_custom_call" | custom-call | flops 10000000000 | bytes 20000000 | tf_op jit(solution)/shard_map/pallas_call | solution.py:567
  164.4 0.0 copy-done.1
  164.4 3.0 %add_convert_fusion = bf16[16,32,1536]{2,1,0:T(8,128)(2,1)} fusion(bf16[16,32,1536]{2,1,0:T(8,128)(2,1)} %get-tuple-element.29, bf16[16,32,1536]{2,1,0:T(8,128)(2,1)S(1)} %copy-done.1), kind=kLoop, calls=%fused_computation | loop fusion | flops 3145728 | bytes 4718592 | tf_op jit(solution)/shard_map/convert_element_type | solution.py:670
  167.4 0.0 copy-start.2
  167.4 5.3 %shard_map.96 = bf16[16,32,1536]{2,1,0:T(8,128)(2,1)} custom-call(bf16[16,32,1536]{2,1,0:T(8,128)(2,1)} %x_ref.3, bf16[16,32,1536]{2,1,0:T(8,128)(2,1)} %get-tuple-element.30.a_ref, bf16[16,32,1536]{2,1,0:T(8,128)(2,1)} %get-tuple-element.31.b_ref), custom_call_target="tpu_custom_call" | custom-call | flops 15728640 | bytes 4718592 | tf_op jit(solution)/shard_map/pallas_call | solution.py:346
  172.7 0.0 copy-done.2
  172.7 0.9 reshape.51
  173.7 0.0 copy-start.5
  173.7 0.0 copy-start.3
  173.7 3.4 %convolution_bitcast_fusion.1 = f32[15,12,8,8]{0,3,2,1:T(8,128)S(1)} fusion(f32[12,8,8,8,8]{4,3,2,1,0:T(8,128)S(1)} %reshape.51, s32[8,8]{1,0:T(8,128)} %copy-done.4), kind=kOutput, calls=%fused_computation.2 | convolution fusion | flops 8848320 | bytes 242944 | tf_op jit(solution)/shard_map/hprqs,pqu,rsv->huv/dot_general | solution.py:673
  177.1 0.0 copy-done.5
  177.1 0.5 convolution_bitcast_fusion.3
  177.6 0.7 reshape.52
  178.3 0.0 copy-done.3
  178.3 0.7 copy.18
  (2 shorter events, 0.0 us)
Async XLA Ops:
  0.6 1.3 copy-start
  1.9 0.6 copy-start.4
  110.4 54.0 %copy-start.1 = (bf16[16,32,1536]{2,1,0:T(8,128)(2,1)S(1)}, bf16[16,32,1536]{2,1,0:T(8,128)(2,1)}, u32[]{:S(2)}) copy-start(bf16[16,32,1536]{2,1,0:T(8,128)(2,1)} %get-tuple-element.23) | copy-start | bytes 4718596
  167.4 5.3 %copy-start.2 = (f32[2,6,64,64]{3,2,1,0:T(8,128)S(1)}, f32[2,6,64,64]{3,2,1,0:T(8,128)}, u32[]{:S(2)}) copy-start(f32[2,6,64,64]{3,2,1,0:T(8,128)} %get-tuple-element.33) | copy-start | bytes 589828
  173.7 3.4 %copy-start.5 = (s32[8,8]{1,0:T(8,128)S(1)}, s32[8,8]{1,0:T(8,128)}, u32[]{:S(2)}) copy-start(s32[8,8]{1,0:T(8,128)} %copy-done.4) | copy-start | bytes 772
  173.7 4.6 %copy-start.3 = (f32[48,1536]{1,0:T(8,128)S(1)}, f32[48,1536]{1,0:T(8,128)}, u32[]{:S(2)}) copy-start(f32[48,1536]{1,0:T(8,128)} %get-tuple-element.40) | copy-start | bytes 884740

commit v5 on v4

--- a/solution.py
+++ b/solution.py
@@ -198,7 +198,6 @@
         )
 
     a_copy = remote(give_ref, agot_ref, tok_send.at[0], tok_recv.at[0], other)
-    a_copy.start()
     quarter = pl.ds(core * 4, 4)
     near = pltpu.make_async_copy(og_ref.at[:, core], held.at[quarter], local)
     far = remote(og_ref.at[:, 1 - core], held.at[quarter], part_send, part_recv, other)
@@ -206,6 +205,7 @@
     far.start()
     near.wait()
     far.wait()
+    a_copy.start()
     place = ring_place(chip)
     sides = (ring_chip(place + 1) * 2 + core, ring_chip(place - 1) * 2 + core)
 

time: 179 us -> 177 us (0.989)
  Pallas kernels: 164 us -> 162 us
    pallas_call x1, Pallas kernels: 54 us -> 51.8 us  [joint_call(): pl.pallas_call(joint_kernel, out_shape=(shape(give.shape, BF16), shape(gi...]
where the time goes in v5:
time: 177 us
  Pallas kernels  162 us (92%)
  matrix products  5.02 us (3%)
  local copies, waits for them, and re-layouts  4.69 us (3%)
  other arithmetic  4.27 us (2%)
    pallas_call x1, Pallas kernels, gathered(): pl.pallas_call(gather_kernel, out_shape=(shape((width, 3 * HALF), BF16),...  66.5 us
    pallas_call x1, Pallas kernels, joint_call(): pl.pallas_call(joint_kernel, out_shape=(shape(give.shape, BF16), shape(gi...  51.8 us
    pallas_call x1, Pallas kernels, shards(): pl.pallas_call(forward_kernel, out_shape=(shape((tokens, 3 * HALF), BF16)...  38.5 us
    pallas_call x1, Pallas kernels, rowwise(): pl.pallas_call(kernel, out_shape=jax.ShapeDtypeStruct(arrays[0].shape, BF...  5.32 us
    dot_general x2, matrix products, shards(): jnp.einsum('hprqs,pqu,rsv->huv', local, table, table, precision=lax.Preci...  3.88 us

profile of v5, /device:TPU:0, one launch (start us, length us, event | category | flops | bytes accessed | tf_op | source)
XLA Modules:
  0.0 176.8 jit_solution(2758404440373631924)
XLA Ops:
  0.6 0.0 copy-start
  0.7 1.2 pad_add_fusion.shifts
  1.9 0.0 copy-done
  1.9 0.0 copy-start.4
  1.9 0.1 reshape.54
  2.0 0.3 convolution_bitcast_fusion.2
  2.3 0.2 copy-done.4
  2.5 0.9 convolution_bitcast_fusion
  3.4 0.1 copy.10
  3.5 0.4 tile.10
  3.9 0.3 tile.11
  4.2 1.2 tile.12.bias_ref
  5.4 66.5 %shard_map.93 = (bf16[1536,1152]{1,0:T(8,128)(2,1)}, bf16[8,2,48,1536]{3,2,1,0:T(8,128)(2,1)}, bf16[2,16,32,1536]{3,2,1,0:T(8,128)(2,1)}, bf16[2,16,32,1536]{3,2,1,0:T(8,128)(2,1)}) custom-call(bf16[96,2304]{1,0:T(8,128)(2,1)} %w_ref.1, bf16[48,1536]{1,0:T(8,128)(2,1)} %ow_ref.1, bf16[16,32,1536]{2,1,0:T(8,128)(2,1)} %x_ref.3, bf16[16,32,1536]{2,1,0:T(8,128)(2,1)} %cot_ref.1), custom_call_target="tpu_custom_call" | custom-call | flops 100000000 | bytes 100000000 | tf_op jit(solution)/shard_map/pallas_call | solution.py:542
  71.9 38.5 %shard_map.94 = (bf16[1024,1152]{1,0:T(8,128)(2,1)}, f32[48,128,128]{2,1,0:T(8,128)}, bf16[1024,384]{1,0:T(8,128)(2,1)}, bf16[16,32,1536]{2,1,0:T(8,128)(2,1)}, ...) custom-call(s32[4]{0:T(128)} %pad_add_fusion.shifts, bf16[32,32,1536]{2,1,0:T(8,128)(2,1)} %bitcast.45, ...), custom_call_target="tpu_custom_call" | custom-call | flops 10000000000 | bytes 20000000 | tf_op jit(solution)/shard_map/pallas_call | solution.py:643
  110.4 0.0 copy-start.1
  110.4 51.8 %shard_map.95 = (bf16[16,32,1536]{2,1,0:T(8,128)(2,1)}, bf16[16,32,1536]{2,1,0:T(8,128)(2,1)}, bf16[16,32,1536]{2,1,0:T(8,128)(2,1)}, f32[48,1536]{1,0:T(8,128)}, f32[2,6,64,64]{3,2,1,0:T(8,128)}) custom-call(s32[4]{0:T(128)} %pad_add_fusion.shifts, bf16[1024,1152]{1,0:T(8,128)(2,1)} %get-tuple-element.24.packed_ref, ...), custom_call_target="tpu_custom_call" | custom-call | flops 10000000000 | bytes 20000000 | tf_op jit(solution)/shard_map/pallas_call | solution.py:567
  162.2 0.0 copy-done.1
  162.2 3.0 %add_convert_fusion = bf16[16,32,1536]{2,1,0:T(8,128)(2,1)} fusion(bf16[16,32,1536]{2,1,0:T(8,128)(2,1)} %get-tuple-element.29, bf16[16,32,1536]{2,1,0:T(8,128)(2,1)S(1)} %copy-done.1), kind=kLoop, calls=%fused_computation | loop fusion | flops 3145728 | bytes 4718592 | tf_op jit(solution)/shard_map/convert_element_type | solution.py:670
  165.2 0.0 copy-start.2
  165.2 5.3 %shard_map.96 = bf16[16,32,1536]{2,1,0:T(8,128)(2,1)} custom-call(bf16[16,32,1536]{2,1,0:T(8,128)(2,1)} %x_ref.3, bf16[16,32,1536]{2,1,0:T(8,128)(2,1)} %get-tuple-element.30.a_ref, bf16[16,32,1536]{2,1,0:T(8,128)(2,1)} %get-tuple-element.31.b_ref), custom_call_target="tpu_custom_call" | custom-call | flops 15728640 | bytes 4718592 | tf_op jit(solution)/shard_map/pallas_call | solution.py:346
  170.6 0.0 copy-done.2
  170.6 0.9 reshape.51
  171.5 0.0 copy-start.5
  171.5 0.0 copy-start.3
  171.5 3.4 %convolution_bitcast_fusion.1 = f32[15,12,8,8]{0,3,2,1:T(8,128)S(1)} fusion(f32[12,8,8,8,8]{4,3,2,1,0:T(8,128)S(1)} %reshape.51, s32[8,8]{1,0:T(8,128)} %copy-done.4), kind=kOutput, calls=%fused_computation.2 | convolution fusion | flops 8848320 | bytes 242944 | tf_op jit(solution)/shard_map/hprqs,pqu,rsv->huv/dot_general | solution.py:673
  174.9 0.0 copy-done.5
  174.9 0.5 convolution_bitcast_fusion.3
  175.4 0.7 reshape.52
  176.1 0.0 copy-done.3
  176.1 0.7 copy.18
  (2 shorter events, 0.0 us)
Async XLA Ops:
  0.6 1.3 copy-start
  1.9 0.6 copy-start.4
  110.4 51.8 %copy-start.1 = (bf16[16,32,1536]{2,1,0:T(8,128)(2,1)S(1)}, bf16[16,32,1536]{2,1,0:T(8,128)(2,1)}, u32[]{:S(2)}) copy-start(bf16[16,32,1536]{2,1,0:T(8,128)(2,1)} %get-tuple-element.23) | copy-start | bytes 4718596
  165.2 5.3 %copy-start.2 = (f32[2,6,64,64]{3,2,1,0:T(8,128)S(1)}, f32[2,6,64,64]{3,2,1,0:T(8,128)}, u32[]{:S(2)}) copy-start(f32[2,6,64,64]{3,2,1,0:T(8,128)} %get-tuple-element.33) | copy-start | bytes 589828
  171.5 3.4 %copy-start.5 = (s32[8,8]{1,0:T(8,128)S(1)}, s32[8,8]{1,0:T(8,128)}, u32[]{:S(2)}) copy-start(s32[8,8]{1,0:T(8,128)} %copy-done.4) | copy-start | bytes 772
  171.5 4.6 %copy-start.3 = (f32[48,1536]{1,0:T(8,128)S(1)}, f32[48,1536]{1,0:T(8,128)}, u32[]{:S(2)}) copy-start(f32[48,1536]{1,0:T(8,128)} %get-tuple-element.40) | copy-start | bytes 884740
